TPU v7x, 128 devices: a whole 4x4x4 slice. The times are simulated.
128 devices in a mesh: row: 8 (over z_hi, y), col: 4 (over z_lo, core), depth: 4 (over x).
Axes of the slice: x: 4, y: 4, z: 4 (z_hi: 2, z_lo: 2; z = z_hi * 2 + z_lo), core: 2. Of those that a mesh axis runs over, the one named last changes fastest.
Arguments:
- tokens: bfloat16 [1024, 14848], P(('row', 'col'), 'depth'), may hold values from -6 to 6
- w_up: bfloat16 [14848, 32768], P('depth', ('row', 'col')), may hold values from -0.046875 to 0.046875
- grad_hidden: bfloat16 [1024, 32768], P('depth', ('row', 'col')), may hold values from -6 to 6
Outputs:
- hidden_act: bfloat16 [1024, 32768], P('depth', ('row', 'col'))
- input_grad: bfloat16 [1024, 14848], P(('row', 'col'), 'depth')
- weight_grad: bfloat16 [14848, 32768], P('depth', ('row', 'col'))
All inputs are finite; a program needn't handle non-finite values.
Results may differ from a plain program's by a relative error of at most 0.0049.
Values may be sent and summed in bfloat16 or wider, within the bound.
No kernel may reach another device: no remote copies, remote signals or barrier semaphores. Data moves between devices by JAX's collectives and lax.ppermute only.
A program may use at most 128 MiB of HBM per device.

v0:
```python
import jax
import jax.numpy as jnp
from jax import lax
from jax.experimental import pallas as pl
from jax.experimental.pallas import tpu as pltpu
from jax.sharding import PartitionSpec as P

root_half = 0.7071067811865476
norm_density = 0.3989422804014327
PLANE = ("row", "col")
f32, bf16 = jnp.float32, jnp.bfloat16


def spot(z, y, core):
    return ((z // 2) * 4 + y) * 4 + (z % 2) * 2 + core


def plane_pairs(leg, way):
    pairs = []
    for z in range(4):
        for y in range(4):
            for core in range(2):
                on_y = (leg == "first") == (core == 0)
                to = ((z, (y + way) % 4) if on_y else ((z + way) % 4, y)) + (core,)
                pairs.append((spot(z, y, core), spot(*to)))
    return pairs


def move(block, leg, way):
    if leg == "depth":
        return lax.ppermute(block, "depth", [(i, (i + way) % 4) for i in range(4)])
    return lax.ppermute(block, PLANE, plane_pairs(leg, way))


def swap(block):
    return lax.ppermute(
        block,
        PLANE,
        [(spot(z, y, c), spot(z, y, 1 - c)) for z in range(4) for y in range(4) for c in range(2)],
    )


def pick(stack, at):
    return lax.dynamic_index_in_dim(stack, at, 0, keepdims=False)


def place(stack, part, at):
    return lax.dynamic_update_slice_in_dim(stack, part[None], at % 4, 0)


def gather_near(block, leg, at):
    whole = jnp.zeros((4,) + block.shape, block.dtype)
    for shift in (0, 1, 2, 3):
        part = move(block, leg, shift) if shift else block
        whole = place(whole, part, at + 4 - shift)
    return whole


def scatter_near(stack, leg, at):
    total = pick(stack, at)
    for shift in (2, 1, 3):
        total += move(pick(stack, (at + shift) % 4).astype(bf16), leg, shift).astype(f32)
    return total


def cross(block, step):
    pairs = []
    for col in range(4):
        for x in range(4):
            pairs.append((col * 4 + x, col * 4 + ((x ^ 1) if (step + col) % 2 == 0 else 3 - x)))
    return lax.ppermute(block, ("col", "depth"), pairs)


def partner(at, core, step):
    return jnp.where((step + core) % 2 == 0, at ^ 1, 3 - at)


def turn_block(after_ref, *refs):
    blocks, out_ref = refs[:-1], refs[-1]
    for i, block in enumerate(blocks):

        @pl.when(pl.program_id(0) == i)
        def _(block=block):
            out_ref[...] = block[...].T


def turn(matrices, after):
    rows, columns = matrices[0].shape
    step = 256
    count = columns // step

    def at(i):
        return lambda m, j: (0, jnp.where(m == i, j, jnp.where(m < i, 0, count - 1)))

    return pl.pallas_call(
        turn_block,
        grid=(len(matrices), count),
        in_specs=[pl.BlockSpec(after.shape, lambda m, j: (0, 0))]
        + [pl.BlockSpec((rows, step), at(i)) for i in range(len(matrices))],
        out_specs=pl.BlockSpec((step, rows), lambda m, j: (m * count + j, 0)),
        out_shape=jax.ShapeDtypeStruct((len(matrices) * columns, rows), matrices[0].dtype),
        compiler_params=pltpu.CompilerParams(vmem_limit_bytes=24 * 2**20),
        cost_estimate=pl.CostEstimate(
            flops=0, bytes_accessed=4 * len(matrices) * rows * columns, transcendentals=0
        ),
    )(after, *matrices)


def hold_block(after_ref, block_ref, out_ref):
    out_ref[...] = block_ref[...]


def hold(matrix, after):
    rows, columns = matrix.shape
    step = 256
    return pl.pallas_call(
        hold_block,
        grid=(columns // step,),
        in_specs=[
            pl.BlockSpec(after.shape, lambda i: (0, 0)),
            pl.BlockSpec((rows, step), lambda i: (0, i)),
        ],
        out_specs=pl.BlockSpec((rows, step), lambda i: (0, i)),
        out_shape=jax.ShapeDtypeStruct(matrix.shape, matrix.dtype),
        compiler_params=pltpu.CompilerParams(vmem_limit_bytes=24 * 2**20),
        cost_estimate=pl.CostEstimate(
            flops=0, bytes_accessed=4 * rows * columns, transcendentals=0
        ),
    )(after, matrix)


def shards(tokens, w_up, grad_hidden):
    row, col, depth = lax.axis_index("row"), lax.axis_index("col"), lax.axis_index("depth")
    z, y, core = (row // 4) * 2 + col // 2, row % 4, col % 2
    first, second = jnp.where(core == 0, y, z), jnp.where(core == 0, z, y)
    share, width = tokens.shape
    hidden = w_up.shape[1]

    def slot(at):
        return jnp.where(core == 0, at % 4, (at % 2) * 2 + (at % 4) // 2)

    def side_order(rows):
        return jnp.where(core == 0, rows.swapaxes(0, 1), rows)

    w_other = swap(w_up)
    cotangent = grad_hidden.reshape(2, 2, 2, share, hidden)
    cotangent_other = swap(lax.dynamic_index_in_dim(cotangent, 1 - core, 2, keepdims=False))
    cotangent = lax.dynamic_index_in_dim(cotangent, core, 2, keepdims=False)

    line = gather_near(tokens, "first", first).reshape(-1, width)
    count = line.shape[0]
    half = count // 2
    below, above = move(line, "second", 1), move(line, "second", -1)
    held = hold(w_other, line[:16, :128])
    held, below, above = tie(held, below, above)
    beyond = jnp.concatenate(
        [move(below[:half], "second", 1), move(above[half:], "second", -1)], 0
    )
    every = jnp.zeros((2, 4) + line.shape, bf16)
    sums = [jnp.zeros((4, count, hidden), f32) for _ in range(2)]
    for shift, part in ((0, line), (3, below), (1, above), (2, beyond)):
        every = lax.dynamic_update_slice(every, part[None, None], (0, (second + shift) % 4, 0, 0))
        every = lax.dynamic_update_slice(
            every, swap(part)[None, None], (1, (first + shift) % 4, 0, 0)
        )
        for i, weight in enumerate((w_up, held)):
            product = jnp.dot(part, weight, preferred_element_type=f32)
            sums[i] = place(sums[i], product, second + shift)

    def split(total):
        rows = total.reshape(2, 2, 2, 2, share, hidden).transpose(0, 2, 1, 3, 4, 5)
        return rows.reshape(4, count, hidden)

    stack = jnp.concatenate([split(total) for total in sums], -1)
    near, mate = partner(depth, core, 0), partner(depth, core, 1)
    near_mate = partner(near, core, 1)
    away = jnp.stack([pick(stack, slot(near)), pick(stack, slot(near_mate))], 0).astype(bf16)
    got = cross(away, 0)
    turned = turn((w_up, held), away[0, :16, :128])
    turned, got = tie(turned, got)
    send = (pick(stack, slot(mate)) + got[1].astype(f32)).astype(bf16)
    pre_act = pick(stack, slot(depth)) + got[0].astype(f32) + cross(send, 1).astype(f32)

    edge = lax.erf(pre_act * root_half)
    act = (0.5 * pre_act * (1.0 + edge)).astype(bf16).reshape(2, 2, share, 2 * hidden)
    slope = 0.5 * (1.0 + edge) + pre_act * norm_density * jnp.exp(-0.5 * pre_act * pre_act)
    cotangent = side_order(jnp.concatenate([cotangent, cotangent_other], -1))
    grad_own = (cotangent.reshape(pre_act.shape).astype(f32) * slope).astype(bf16)

    lower, upper = move(grad_own, "depth", 1), move(grad_own, "depth", -1)
    middle = count // 2
    opposite = jnp.concatenate(
        [move(lower[:middle], "depth", 1), move(upper[middle:], "depth", -1)], 0
    )
    grads = jnp.zeros((4,) + grad_own.shape, bf16)
    for shift, part in ((0, grad_own), (3, lower), (1, upper), (2, opposite)):
        grads = place(grads, part, slot(depth + shift))
    grads = grads.reshape(2, 2, 2, 2 * share, 2 * hidden)

    def piece_of(grads, shift):
        at = (second + shift) % 4
        return lax.dynamic_slice(
            grads, (at // 2, 0, at % 2, 0, 0), (1, 2, 1) + grads.shape[3:]
        ).reshape(count, 2 * hidden)

    far = jnp.dot(piece_of(grads, 2), turned, preferred_element_type=f32).astype(bf16)
    far, grads = tie(far, grads)
    low, high = move(far[:half], "second", 1), move(far[half:], "second", -1)
    rest = jnp.concatenate([piece_of(grads, shift) for shift in (1, 3, 0)], 0)
    rest = jnp.dot(rest, turned, preferred_element_type=f32)
    up, down, ours = rest[:count], rest[count : 2 * count], rest[2 * count :]
    up = jnp.concatenate([up[:half] + low.astype(f32), up[half:]], 0).astype(bf16)
    down = jnp.concatenate([down[:half], down[half:] + high.astype(f32)], 0).astype(bf16)

    order = grads.transpose(0, 2, 1, 3, 4).reshape(16 * share, 2 * hidden)
    beside = jnp.concatenate([order[:, :hidden], swap(order[:, hidden:])], 0)
    flat = every.reshape(-1, width)
    up, down, beside, flat = tie(up, down, beside, flat)
    from_below, from_above = move(up, "second", 1), move(down, "second", -1)
    weight_grad = lax.dot_general(
        flat, beside, (((0,), (0,)), ((), ())), preferred_element_type=f32
    ).astype(bf16)
    weight_grad, ours, from_below, from_above = tie(weight_grad, ours, from_below, from_above)
    ours = ours + from_below.astype(f32) + from_above.astype(f32)
    input_grad = scatter_near(ours.reshape(4, share, width), "first", first).astype(bf16)

    act_own, act_other = side_order(act[..., :hidden]), swap(side_order(act[..., hidden:]))
    hidden_act = jnp.stack(
        [jnp.where(core == 0, act_own, act_other), jnp.where(core == 0, act_other, act_own)], 2
    )
    return hidden_act.reshape(-1, hidden), input_grad, weight_grad


def tie(*values):
    return lax.optimization_barrier(values)


def solution(mesh):
    placed = (P(PLANE, "depth"), P("depth", PLANE), P("depth", PLANE))
    return jax.shard_map(
        shards,
        mesh=mesh,
        in_specs=placed,
        out_specs=(P("depth", PLANE), P(PLANE, "depth"), P("depth", PLANE)),
        check_vma=False,
    )
```

profile of v0, /device:TPU:1, one launch (start us, length us, event | category | flops | bytes accessed | tf_op | source)
XLA Modules:
  0.0 145.6 jit_solution(872705687583951983)
XLA Ops:
  0.6 1.5 %collective-permute-start.3 = (bf16[3712,1024]{1,0:T(8,128)(2,1)}, bf16[3712,1024]{1,0:T(8,128)(2,1)}, u32[]{:S(2)}, u32[]{:S(2)}) collective-permute-start(bf16[3712,1024]{1,0:T(8,128)(2,1)} %refs_0_.1), channel_id=1, source_target_pairs={{0,4},{4,0},{16,20},{20,16},{32,36},{36,32},{48,52},{52,48},{8,12}... | collective-permute-start | bytes 22806536 | tf_op jit(solution)/shard_map/ppermute | solution.py:36
  2.1 1.7 %collective-permute-start = (bf16[32,3712]{1,0:T(8,128)(2,1)}, bf16[32,3712]{1,0:T(8,128)(2,1)S(1)}, u32[]{:S(2)}, u32[]{:S(2)}) collective-permute-start(bf16[32,3712]{1,0:T(8,128)(2,1)} %param.3), channel_id=1, source_target_pairs={{0,16},{4,12},{16,32},{20,28},{32,48},{36,44},{48,0},{52,60},{8,24... | collective-permute-start | bytes 712712 | tf_op jit(solution)/shard_map/ppermute | solution.py:32
  3.9 3.3 %collective-permute-start.1 = (bf16[32,3712]{1,0:T(8,128)(2,1)}, bf16[32,3712]{1,0:T(8,128)(2,1)S(1)}, u32[]{:S(2)}, u32[]{:S(2)}) collective-permute-start(bf16[32,3712]{1,0:T(8,128)(2,1)} %param.3), channel_id=1, source_target_pairs={{0,32},{4,68},{16,48},{20,84},{32,0},{36,100},{48,16},{52,116},{8,... | collective-permute-start | bytes 712712 | tf_op jit(solution)/shard_map/ppermute | solution.py:32
  11.2 2.2 %collective-permute-done.1 = bf16[32,3712]{1,0:T(8,128)(2,1)S(1)} collective-permute-done((bf16[32,3712]{1,0:T(8,128)(2,1)}, bf16[32,3712]{1,0:T(8,128)(2,1)S(1)}, u32[]{:S(2)}, u32[]{:S(2)}) %collective-permute-start.1) | collective-permute-done | bytes 237600 | tf_op jit(solution)/shard_map/ppermute | solution.py:32
  13.5 1.4 collective-permute-start.4
  14.8 1.5 %collective-permute-start.5 = (bf16[128,3712]{1,0:T(8,128)(2,1)S(1)}, bf16[128,3712]{1,0:T(8,128)(2,1)S(1)}, u32[]{:S(2)}, u32[]{:S(2)}) collective-permute-start(bf16[128,3712]{1,0:T(8,128)(2,1)S(1)} %bitcast.157), channel_id=1, source_target_pairs={{0,72},{4,52},{16,88},{20,4},{32,104},{36,20},{48,120},{52,36},{8,... | collective-permute-start | bytes 2850824 | tf_op jit(solution)/shard_map/ppermute | solution.py:32
  16.4 1.5 %collective-permute-start.19 = (bf16[128,3712]{1,0:T(8,128)(2,1)S(1)}, bf16[128,3712]{1,0:T(8,128)(2,1)S(1)}, u32[]{:S(2)}, u32[]{:S(2)}) collective-permute-start(bf16[128,3712]{1,0:T(8,128)(2,1)S(1)} %bitcast.158), channel_id=1, source_target_pairs={{0,4},{4,0},{16,20},{20,16},{32,36},{36,32},{48,52},{52,48},{8,12}... | collective-permute-start | bytes 2850824 | tf_op jit(solution)/shard_map/ppermute | solution.py:36
  18.1 4.3 %fusion.13 = f32[4,128,1024]{2,1,0:T(8,128)S(1)} fusion(f32[4,128,1024]{2,1,0:T(8,128)S(1)} %broadcast.60.clone, s32[]{:T(128)S(6)} %select_n.424, bf16[128,3712]{1,0:T(8,128)(2,1)S(1)} %bitcast.159, bf16[3712,1024]{1,0:T(8,128)(2,1)} %refs_0_.1), kind=kOutput, calls=%fused_computation.34 | convolution fusion | flops 973078528 | bytes 9076740 | tf_op jit(solution)/shard_map/dot_general | solution.py:167
  23.4 5.8 %shard_map.58.refs_1_ = bf16[3712,1024]{1,0:T(8,128)(2,1)S(1)} custom-call(bf16[16,128]{1,0:T(8,128)(2,1)S(1)} %slice.85.after_ref, bf16[3712,1024]{1,0:T(8,128)(2,1)} %collective-permute-done.3.block_ref), custom_call_target="tpu_custom_call" | custom-call | bytes 15204352 | tf_op jit(solution)/shard_map/pallas_call | solution.py:116
  31.3 1.4 collective-permute-start.7
  37.8 1.9 %copy-done.1 = bf16[2,4,128,3712]{3,2,1,0:T(8,128)(2,1)} copy-done((bf16[2,4,128,3712]{3,2,1,0:T(8,128)(2,1)}, bf16[2,4,128,3712]{3,2,1,0:T(8,128)(2,1)S(1)}, u32[]{:S(2)}) %copy-start.1) | copy-done | bytes 7602200
  45.0 6.6 %shard_map.59 = bf16[2048,3712]{1,0:T(8,128)(2,1)S(1)} custom-call(bf16[16,128]{1,0:T(8,128)(2,1)S(1)} %slice_bitcast_fusion.1.after_ref, bf16[3712,1024]{1,0:T(8,128)(2,1)S(1)} %bitcast.149, bf16[3712,1024]{1,0:T(8,128)(2,1)S(1)} %shard_map.58.refs_1_), custom_call_target="tpu_custom_call" | custom-call | bytes 30408704 | tf_op jit(solution)/shard_map/pallas_call | solution.py:95
  51.7 2.6 %collective-permute-start.8 = (bf16[2,128,2048]{2,1,0:T(8,128)(2,1)S(1)}, bf16[2,128,2048]{2,1,0:T(8,128)(2,1)S(1)}, u32[]{:S(2)}, u32[]{:S(2)}) collective-permute-start(bf16[2,128,2048]{2,1,0:T(8,128)(2,1)S(1)} %pad_maximum_fusion.1), channel_id=1, source_target_pairs={{0,1},{1,0},{2,3},{3,2},{4,7},{5,6},{6,5},{7,4},{8,9},{9,8},{10,11... | collective-permute-start | bytes 3145736 | tf_op jit(solution)/shard_map/ppermute | solution.py:71
  54.3 1.7 %bitcast_dynamic-update-slice_fusion.4 = bf16[2,4,128,3712]{3,2,1,0:T(8,128)(2,1)} fusion(bf16[2,4,128,3712]{3,2,1,0:T(8,128)(2,1)} %copy-done.1, s32[]{:T(128)S(6)} %select_n.417, bf16[128,3712]{1,0:T(8,128)(2,1)S(1)} %collective-permute-done.20), kind=kLoop, calls=%fused_computation.64 | loop fusion | bytes 1900548 | tf_op jit(solution)/shard_map/dynamic_update_slice | solution.py:163
  56.0 1.8 %bitcast_dynamic-update-slice_fusion.3 = bf16[2,4,128,3712]{3,2,1,0:T(8,128)(2,1)} fusion(bf16[2,4,128,3712]{3,2,1,0:T(8,128)(2,1)} %bitcast_dynamic-update-slice_fusion.4, s32[]{:T(128)S(6)} %select_n.428, bf16[128,3712]{1,0:T(8,128)(2,1)S(1)} %collective-permute-done.5), kind=kLoop, calls=%fused_computation.63 | loop fusion | bytes 1900548 | tf_op jit(solution)/shard_map/dynamic_update_slice | solution.py:162
  59.8 6.8 %collective-permute-done.8 = bf16[2,128,2048]{2,1,0:T(8,128)(2,1)S(1)} collective-permute-done((bf16[2,128,2048]{2,1,0:T(8,128)(2,1)S(1)}, bf16[2,128,2048]{2,1,0:T(8,128)(2,1)S(1)}, u32[]{:S(2)}, u32[]{:S(2)}) %collective-permute-start.8) | collective-permute-done | bytes 1048608 | tf_op jit(solution)/shard_map/ppermute | solution.py:71
  67.2 2.2 %bitcast_dynamic-update-slice_fusion = bf16[2,4,128,3712]{3,2,1,0:T(8,128)(2,1)} fusion(bf16[2,4,128,3712]{3,2,1,0:T(8,128)(2,1)} %bitcast_dynamic-update-slice_fusion.1, s32[]{:T(128)S(6)} %select_n.419, bf16[128,3712]{1,0:T(8,128)(2,1)} %collective-permute-done.22), kind=kLoop, calls=%fused_computation.60 | loop fusion | bytes 1900548 | tf_op jit(solution)/shard_map/dynamic_update_slice | solution.py:163
  69.4 5.8 %collective-permute-done.9 = bf16[128,2048]{1,0:T(8,128)(2,1)S(1)} collective-permute-done((bf16[128,2048]{1,0:T(8,128)(2,1)S(1)}, bf16[128,2048]{1,0:T(8,128)(2,1)S(1)}, u32[]{:S(2)}, u32[]{:S(2)}) %collective-permute-start.9) | collective-permute-done | bytes 524320 | tf_op jit(solution)/shard_map/ppermute | solution.py:71
  76.4 2.4 %collective-permute-start.13 = (bf16[128,2048]{1,0:T(8,128)(2,1)S(1)}, bf16[128,2048]{1,0:T(8,128)(2,1)S(1)}, u32[]{:S(2)}, u32[]{:S(2)}) collective-permute-start(bf16[128,2048]{1,0:T(8,128)(2,1)S(1)} %get-tuple-element.33), channel_id=1, source_target_pairs={{0,3},{1,0},{2,1},{3,2},{4,7},{5,4},{6,5},{7,6},{8,11},{9,8},{10,9... | collective-permute-start | bytes 1572872 | tf_op jit(solution)/shard_map/ppermute | solution.py:31
  79.1 2.7 %collective-permute-start.10 = (bf16[2,2,32,1024]{3,2,1,0:T(8,128)(2,1)S(1)}, bf16[2,2,32,1024]{3,2,1,0:T(8,128)(2,1)S(1)}, u32[]{:S(2)}, u32[]{:S(2)}) collective-permute-start(bf16[2,2,32,1024]{3,2,1,0:T(8,128)(2,1)S(1)} %bitcast_select_fusion), channel_id=1, source_target_pairs={{0,4},{4,0},{16,20},{20,16},{32,36},{36,32},{48,52},{52,48},{8,12}... | collective-permute-start | bytes 786440 | tf_op jit(solution)/shard_map/ppermute | solution.py:36
  82.1 6.0 %collective-permute-done.13 = bf16[128,2048]{1,0:T(8,128)(2,1)S(1)} collective-permute-done((bf16[128,2048]{1,0:T(8,128)(2,1)S(1)}, bf16[128,2048]{1,0:T(8,128)(2,1)S(1)}, u32[]{:S(2)}, u32[]{:S(2)}) %collective-permute-start.13) | collective-permute-done | bytes 524320 | tf_op jit(solution)/shard_map/ppermute | solution.py:31
  88.1 3.1 %collective-permute-start.15 = (bf16[64,2048]{1,0:T(8,128)(2,1)S(1)}, bf16[64,2048]{1,0:T(8,128)(2,1)S(1)}, u32[]{:S(2)}, u32[]{:S(2)}) collective-permute-start(bf16[64,2048]{1,0:T(8,128)(2,1)S(1)} %slice.90), channel_id=1, source_target_pairs={{0,3},{1,0},{2,1},{3,2},{4,7},{5,4},{6,5},{7,6},{8,11},{9,8},{10,9... | collective-permute-start | bytes 786440 | tf_op jit(solution)/shard_map/ppermute | solution.py:31
  91.4 3.1 %collective-permute-done.15 = bf16[64,2048]{1,0:T(8,128)(2,1)S(1)} collective-permute-done((bf16[64,2048]{1,0:T(8,128)(2,1)S(1)}, bf16[64,2048]{1,0:T(8,128)(2,1)S(1)}, u32[]{:S(2)}, u32[]{:S(2)}) %collective-permute-start.15) | collective-permute-done | bytes 262176 | tf_op jit(solution)/shard_map/ppermute | solution.py:31
  94.5 3.2 %collective-permute-done.14 = bf16[64,2048]{1,0:T(8,128)(2,1)S(1)} collective-permute-done((bf16[64,2048]{1,0:T(8,128)(2,1)S(1)}, bf16[64,2048]{1,0:T(8,128)(2,1)S(1)}, u32[]{:S(2)}, u32[]{:S(2)}) %collective-permute-start.14) | collective-permute-done | bytes 262176 | tf_op jit(solution)/shard_map/ppermute | solution.py:31
  97.9 2.2 %convolution_convert_fusion.1 = bf16[128,3712]{1,0:T(8,128)(2,1)S(1)} fusion(bf16[128,2048]{1,0:T(8,128)(2,1)S(1)} %bitcast.176, bf16[2048,3712]{1,0:T(8,128)(2,1)S(1)} %shard_map.59), kind=kOutput, calls=%fused_computation.9 | convolution fusion | flops 1946632192 | bytes 16678912 | tf_op jit(solution)/shard_map/dot_general | solution.py:206
  100.2 2.0 %collective-permute-start.17 = (bf16[64,3712]{1,0:T(8,128)(2,1)S(1)}, bf16[64,3712]{1,0:T(8,128)(2,1)S(1)}, u32[]{:S(2)}, u32[]{:S(2)}) collective-permute-start(bf16[64,3712]{1,0:T(8,128)(2,1)S(1)} %get-tuple-element.51), channel_id=1, source_target_pairs={{0,72},{4,52},{16,88},{20,4},{32,104},{36,20},{48,120},{52,36},{8,... | collective-permute-start | bytes 1425416 | tf_op jit(solution)/shard_map/ppermute | solution.py:32
  102.7 5.0 %collective-permute-start.18 = (bf16[512,1024]{1,0:T(8,128)(2,1)S(1)}, bf16[512,1024]{1,0:T(8,128)(2,1)S(1)}, u32[]{:S(2)}, u32[]{:S(2)}) collective-permute-start(bf16[512,1024]{1,0:T(8,128)(2,1)S(1)} %get-tuple-element.42), channel_id=1, source_target_pairs={{0,4},{4,0},{16,20},{20,16},{32,36},{36,32},{48,52},{52,48},{8,12}... | collective-permute-start | bytes 3145736 | tf_op jit(solution)/shard_map/ppermute | solution.py:36
  107.8 9.5 %fusion.46 = (bf16[384,3712]{1,0:T(8,128)(2,1)S(1)}, f32[384,3712]{1,0:T(8,128)S(1)}) fusion(bf16[2048,3712]{1,0:T(8,128)(2,1)} %copy-done, bf16[128,2048]{1,0:T(8,128)(2,1)S(1)} %bitcast.178, bf16[128,2048]{1,0:T(8,128)(2,1)S(1)} %bitcast.179, bf16[128,2048]{1,0:T(8,128)(2,1)S(1)} %bitcast.177), kind=kOutput, calls=%fused_computation.110 | convolution fusion | flops 5844615168 | bytes 25329664 | tf_op jit(solution)/shard_map/dot_general | solution.py:210
  119.3 1.6 %collective-permute-start.24 = (bf16[128,3712]{1,0:T(8,128)(2,1)S(1)}, bf16[128,3712]{1,0:T(8,128)(2,1)S(1)}, u32[]{:S(2)}, u32[]{:S(2)}) collective-permute-start(bf16[128,3712]{1,0:T(8,128)(2,1)S(1)} %get-tuple-element.28), channel_id=1, source_target_pairs={{0,72},{4,52},{16,88},{20,4},{32,104},{36,20},{48,120},{52,36},{8,... | collective-permute-start | bytes 2850824 | tf_op jit(solution)/shard_map/ppermute | solution.py:32
  120.9 10.5 %convolution_convert_fusion = bf16[3712,1024]{1,0:T(8,128)(2,1)} fusion(bf16[1024,3712]{1,0:T(8,128)(2,1)S(1)} %bitcast.171, bf16[1024,1024]{1,0:T(8,128)(2,1)S(1)} %pad_maximum_fusion), kind=kOutput, calls=%fused_computation | convolution fusion | flops 7788429312 | bytes 17301504 | tf_op jit(solution)/shard_map/dot_general | solution.py:220
  132.8 3.0 %collective-permute-start.27 = (bf16[32,3712]{1,0:T(8,128)(2,1)S(1)}, bf16[32,3712]{1,0:T(8,128)(2,1)S(1)}, u32[]{:S(2)}, u32[]{:S(2)}) collective-permute-start(bf16[32,3712]{1,0:T(8,128)(2,1)S(1)} %get-tuple-element.47), channel_id=1, source_target_pairs={{0,48},{4,76},{16,0},{20,92},{32,16},{36,108},{48,32},{52,124},{8,... | collective-permute-start | bytes 712712 | tf_op jit(solution)/shard_map/ppermute | solution.py:32
  138.8 6.0 %collective-permute-done.26 = bf16[32,3712]{1,0:T(8,128)(2,1)S(1)} collective-permute-done((bf16[32,3712]{1,0:T(8,128)(2,1)S(1)}, bf16[32,3712]{1,0:T(8,128)(2,1)S(1)}, u32[]{:S(2)}, u32[]{:S(2)}) %collective-permute-start.26) | collective-permute-done | bytes 237600 | tf_op jit(solution)/shard_map/ppermute | solution.py:32
  (107 shorter events, 29.1 us)
Async XLA Ops:
  0.6 22.8 %collective-permute-start.3 = (bf16[3712,1024]{1,0:T(8,128)(2,1)}, bf16[3712,1024]{1,0:T(8,128)(2,1)}, u32[]{:S(2)}, u32[]{:S(2)}) collective-permute-start(bf16[3712,1024]{1,0:T(8,128)(2,1)} %refs_0_.1), channel_id=1, source_target_pairs={{0,4},{4,0},{16,20},{20,16},{32,36},{36,32},{48,52},{52,48},{8,12}... | collective-permute-start | bytes 22806536 | tf_op jit(solution)/shard_map/ppermute | solution.py:36
  2.1 9.0 %collective-permute-start = (bf16[32,3712]{1,0:T(8,128)(2,1)}, bf16[32,3712]{1,0:T(8,128)(2,1)S(1)}, u32[]{:S(2)}, u32[]{:S(2)}) collective-permute-start(bf16[32,3712]{1,0:T(8,128)(2,1)} %param.3), channel_id=1, source_target_pairs={{0,16},{4,12},{16,32},{20,28},{32,48},{36,44},{48,0},{52,60},{8,24... | collective-permute-start | bytes 712712 | tf_op jit(solution)/shard_map/ppermute | solution.py:32
  3.9 9.6 %collective-permute-start.1 = (bf16[32,3712]{1,0:T(8,128)(2,1)}, bf16[32,3712]{1,0:T(8,128)(2,1)S(1)}, u32[]{:S(2)}, u32[]{:S(2)}) collective-permute-start(bf16[32,3712]{1,0:T(8,128)(2,1)} %param.3), channel_id=1, source_target_pairs={{0,32},{4,68},{16,48},{20,84},{32,0},{36,100},{48,16},{52,116},{8,... | collective-permute-start | bytes 712712 | tf_op jit(solution)/shard_map/ppermute | solution.py:32
  7.2 6.3 %collective-permute-start.2 = (bf16[32,3712]{1,0:T(8,128)(2,1)}, bf16[32,3712]{1,0:T(8,128)(2,1)S(1)}, u32[]{:S(2)}, u32[]{:S(2)}) collective-permute-start(bf16[32,3712]{1,0:T(8,128)(2,1)} %param.3), channel_id=1, source_target_pairs={{0,48},{4,76},{16,0},{20,92},{32,16},{36,108},{48,32},{52,124},{8,... | collective-permute-start | bytes 712712 | tf_op jit(solution)/shard_map/ppermute | solution.py:32
  9.0 14.2 %collective-permute-start.11 = (bf16[2,2,32,1024]{3,2,1,0:T(8,128)(2,1)S(1)}, bf16[2,2,32,1024]{3,2,1,0:T(8,128)(2,1)S(1)}, u32[]{:S(2)}, u32[]{:S(2)}) collective-permute-start(bf16[2,2,32,1024]{3,2,1,0:T(8,128)(2,1)S(1)} %get-tuple-element.56), channel_id=1, source_target_pairs={{0,4},{4,0},{16,20},{20,16},{32,36},{36,32},{48,52},{52,48},{8,12}... | collective-permute-start | bytes 786440 | tf_op jit(solution)/shard_map/ppermute | solution.py:36
  13.5 15.7 %collective-permute-start.4 = (bf16[128,3712]{1,0:T(8,128)(2,1)S(1)}, bf16[128,3712]{1,0:T(8,128)(2,1)S(1)}, u32[]{:S(2)}, u32[]{:S(2)}) collective-permute-start(bf16[128,3712]{1,0:T(8,128)(2,1)S(1)} %bitcast.156), channel_id=1, source_target_pairs={{0,8},{4,20},{16,24},{20,36},{32,40},{36,52},{48,56},{52,4},{8,64}... | collective-permute-start | bytes 2850824 | tf_op jit(solution)/shard_map/ppermute | solution.py:32
  14.8 14.3 %collective-permute-start.5 = (bf16[128,3712]{1,0:T(8,128)(2,1)S(1)}, bf16[128,3712]{1,0:T(8,128)(2,1)S(1)}, u32[]{:S(2)}, u32[]{:S(2)}) collective-permute-start(bf16[128,3712]{1,0:T(8,128)(2,1)S(1)} %bitcast.157), channel_id=1, source_target_pairs={{0,72},{4,52},{16,88},{20,4},{32,104},{36,20},{48,120},{52,36},{8,... | collective-permute-start | bytes 2850824 | tf_op jit(solution)/shard_map/ppermute | solution.py:32
  16.4 6.9 %collective-permute-start.19 = (bf16[128,3712]{1,0:T(8,128)(2,1)S(1)}, bf16[128,3712]{1,0:T(8,128)(2,1)S(1)}, u32[]{:S(2)}, u32[]{:S(2)}) collective-permute-start(bf16[128,3712]{1,0:T(8,128)(2,1)S(1)} %bitcast.158), channel_id=1, source_target_pairs={{0,4},{4,0},{16,20},{20,16},{32,36},{36,32},{48,52},{52,48},{8,12}... | collective-permute-start | bytes 2850824 | tf_op jit(solution)/shard_map/ppermute | solution.py:36
  23.2 9.4 %slice-start = ((s8[7602176]{0:T(1024)(128)(4,1)}), s8[4194304]{0:T(1024)(128)(4,1)S(1)}, s32[]{:S(2)}) async-start(s8[7602176]{0:T(1024)(128)(4,1)} %bitcast.148), calls=%async_computation | async-start | bytes 8388608
  23.4 9.2 %slice-start.1 = ((s8[7602176]{0:T(1024)(128)(4,1)}), s8[3407872]{0:T(1024)(128)(4,1)S(1)}, s32[]{:S(2)}) async-start(s8[7602176]{0:T(1024)(128)(4,1)} %bitcast.148), calls=%async_computation.1 | async-start | bytes 6815744
  29.2 25.0 %collective-permute-start.20 = (bf16[128,3712]{1,0:T(8,128)(2,1)S(1)}, bf16[128,3712]{1,0:T(8,128)(2,1)S(1)}, u32[]{:S(2)}, u32[]{:S(2)}) collective-permute-start(bf16[128,3712]{1,0:T(8,128)(2,1)S(1)} %collective-permute-done.4), channel_id=1, source_target_pairs={{0,4},{4,0},{16,20},{20,16},{32,36},{36,32},{48,52},{52,48},{8,12}... | collective-permute-start | bytes 2850824 | tf_op jit(solution)/shard_map/ppermute | solution.py:36
  29.7 28.1 %collective-permute-start.21 = (bf16[128,3712]{1,0:T(8,128)(2,1)S(1)}, bf16[128,3712]{1,0:T(8,128)(2,1)S(1)}, u32[]{:S(2)}, u32[]{:S(2)}) collective-permute-start(bf16[128,3712]{1,0:T(8,128)(2,1)S(1)} %collective-permute-done.5), channel_id=1, source_target_pairs={{0,4},{4,0},{16,20},{20,16},{32,36},{36,32},{48,52},{52,48},{8,12}... | collective-permute-start | bytes 2850824 | tf_op jit(solution)/shard_map/ppermute | solution.py:36
  29.9 11.0 %collective-permute-start.6 = (bf16[64,3712]{1,0:T(8,128)(2,1)S(1)}, bf16[64,3712]{1,0:T(8,128)(2,1)S(1)}, u32[]{:S(2)}, u32[]{:S(2)}) collective-permute-start(bf16[64,3712]{1,0:T(8,128)(2,1)S(1)} %slice.67), channel_id=1, source_target_pairs={{0,8},{4,20},{16,24},{20,36},{32,40},{36,52},{48,56},{52,4},{8,64}... | collective-permute-start | bytes 1425416 | tf_op jit(solution)/shard_map/ppermute | solution.py:32
  31.3 9.7 %collective-permute-start.7 = (bf16[64,3712]{1,0:T(8,128)(2,1)S(1)}, bf16[64,3712]{1,0:T(8,128)(2,1)S(1)}, u32[]{:S(2)}, u32[]{:S(2)}) collective-permute-start(bf16[64,3712]{1,0:T(8,128)(2,1)S(1)} %slice.68), channel_id=1, source_target_pairs={{0,72},{4,52},{16,88},{20,4},{32,104},{36,20},{48,120},{52,36},{8,... | collective-permute-start | bytes 1425416 | tf_op jit(solution)/shard_map/ppermute | solution.py:32
  41.0 26.2 %collective-permute-start.22 = (bf16[128,3712]{1,0:T(8,128)(2,1)S(1)}, bf16[128,3712]{1,0:T(8,128)(2,1)}, u32[]{:S(2)}, u32[]{:S(2)}) collective-permute-start(bf16[128,3712]{1,0:T(8,128)(2,1)S(1)} %constant_dynamic-update-slice_fusion.1), channel_id=1, source_target_pairs={{0,4},{4,0},{16,20},{20,16},{32,36},{36,32},{48,52},{52,48},{8,12}... | collective-permute-start | bytes 2850824 | tf_op jit(solution)/shard_map/ppermute | solution.py:36
  51.6 46.3 %copy-start = (bf16[2048,3712]{1,0:T(8,128)(2,1)}, bf16[2048,3712]{1,0:T(8,128)(2,1)S(1)}, u32[]{:S(2)}) copy-start(bf16[2048,3712]{1,0:T(8,128)(2,1)S(1)} %shard_map.59) | copy-start | bytes 45613060
  51.7 14.9 %collective-permute-start.8 = (bf16[2,128,2048]{2,1,0:T(8,128)(2,1)S(1)}, bf16[2,128,2048]{2,1,0:T(8,128)(2,1)S(1)}, u32[]{:S(2)}, u32[]{:S(2)}) collective-permute-start(bf16[2,128,2048]{2,1,0:T(8,128)(2,1)S(1)} %pad_maximum_fusion.1), channel_id=1, source_target_pairs={{0,1},{1,0},{2,3},{3,2},{4,7},{5,6},{6,5},{7,4},{8,9},{9,8},{10,11... | collective-permute-start | bytes 3145736 | tf_op jit(solution)/shard_map/ppermute | solution.py:71
  66.8 8.4 %collective-permute-start.9 = (bf16[128,2048]{1,0:T(8,128)(2,1)S(1)}, bf16[128,2048]{1,0:T(8,128)(2,1)S(1)}, u32[]{:S(2)}, u32[]{:S(2)}) collective-permute-start(bf16[128,2048]{1,0:T(8,128)(2,1)S(1)} %fusion.33), channel_id=1, source_target_pairs={{0,3},{1,2},{2,1},{3,0},{4,5},{5,4},{6,7},{7,6},{8,11},{9,10},{10,... | collective-permute-start | bytes 1572872 | tf_op jit(solution)/shard_map/ppermute | solution.py:71
  75.8 15.4 %collective-permute-start.12 = (bf16[128,2048]{1,0:T(8,128)(2,1)S(1)}, bf16[128,2048]{1,0:T(8,128)(2,1)S(1)}, u32[]{:S(2)}, u32[]{:S(2)}) collective-permute-start(bf16[128,2048]{1,0:T(8,128)(2,1)S(1)} %get-tuple-element.33), channel_id=1, source_target_pairs={{0,1},{1,2},{2,3},{3,0},{4,5},{5,6},{6,7},{7,4},{8,9},{9,10},{10,1... | collective-permute-start | bytes 1572872 | tf_op jit(solution)/shard_map/ppermute | solution.py:31
  76.4 11.7 %collective-permute-start.13 = (bf16[128,2048]{1,0:T(8,128)(2,1)S(1)}, bf16[128,2048]{1,0:T(8,128)(2,1)S(1)}, u32[]{:S(2)}, u32[]{:S(2)}) collective-permute-start(bf16[128,2048]{1,0:T(8,128)(2,1)S(1)} %get-tuple-element.33), channel_id=1, source_target_pairs={{0,3},{1,0},{2,1},{3,2},{4,7},{5,4},{6,5},{7,6},{8,11},{9,8},{10,9... | collective-permute-start | bytes 1572872 | tf_op jit(solution)/shard_map/ppermute | solution.py:31
  79.1 58.0 %collective-permute-start.10 = (bf16[2,2,32,1024]{3,2,1,0:T(8,128)(2,1)S(1)}, bf16[2,2,32,1024]{3,2,1,0:T(8,128)(2,1)S(1)}, u32[]{:S(2)}, u32[]{:S(2)}) collective-permute-start(bf16[2,2,32,1024]{3,2,1,0:T(8,128)(2,1)S(1)} %bitcast_select_fusion), channel_id=1, source_target_pairs={{0,4},{4,0},{16,20},{20,16},{32,36},{36,32},{48,52},{52,48},{8,12}... | collective-permute-start | bytes 786440 | tf_op jit(solution)/shard_map/ppermute | solution.py:36
  88.1 6.4 %collective-permute-start.15 = (bf16[64,2048]{1,0:T(8,128)(2,1)S(1)}, bf16[64,2048]{1,0:T(8,128)(2,1)S(1)}, u32[]{:S(2)}, u32[]{:S(2)}) collective-permute-start(bf16[64,2048]{1,0:T(8,128)(2,1)S(1)} %slice.90), channel_id=1, source_target_pairs={{0,3},{1,0},{2,1},{3,2},{4,7},{5,4},{6,5},{7,6},{8,11},{9,8},{10,9... | collective-permute-start | bytes 786440 | tf_op jit(solution)/shard_map/ppermute | solution.py:31
  91.2 6.5 %collective-permute-start.14 = (bf16[64,2048]{1,0:T(8,128)(2,1)S(1)}, bf16[64,2048]{1,0:T(8,128)(2,1)S(1)}, u32[]{:S(2)}, u32[]{:S(2)}) collective-permute-start(bf16[64,2048]{1,0:T(8,128)(2,1)S(1)} %slice.89), channel_id=1, source_target_pairs={{0,1},{1,2},{2,3},{3,0},{4,5},{5,6},{6,7},{7,4},{8,9},{9,10},{10,1... | collective-permute-start | bytes 786440 | tf_op jit(solution)/shard_map/ppermute | solution.py:31
  100.2 17.4 %collective-permute-start.17 = (bf16[64,3712]{1,0:T(8,128)(2,1)S(1)}, bf16[64,3712]{1,0:T(8,128)(2,1)S(1)}, u32[]{:S(2)}, u32[]{:S(2)}) collective-permute-start(bf16[64,3712]{1,0:T(8,128)(2,1)S(1)} %get-tuple-element.51), channel_id=1, source_target_pairs={{0,72},{4,52},{16,88},{20,4},{32,104},{36,20},{48,120},{52,36},{8,... | collective-permute-start | bytes 1425416 | tf_op jit(solution)/shard_map/ppermute | solution.py:32
  102.2 15.4 %collective-permute-start.16 = (bf16[64,3712]{1,0:T(8,128)(2,1)S(1)}, bf16[64,3712]{1,0:T(8,128)(2,1)S(1)}, u32[]{:S(2)}, u32[]{:S(2)}) collective-permute-start(bf16[64,3712]{1,0:T(8,128)(2,1)S(1)} %get-tuple-element.52), channel_id=1, source_target_pairs={{0,8},{4,20},{16,24},{20,36},{32,40},{36,52},{48,56},{52,4},{8,64}... | collective-permute-start | bytes 1425416 | tf_op jit(solution)/shard_map/ppermute | solution.py:32
  102.7 15.3 %collective-permute-start.18 = (bf16[512,1024]{1,0:T(8,128)(2,1)S(1)}, bf16[512,1024]{1,0:T(8,128)(2,1)S(1)}, u32[]{:S(2)}, u32[]{:S(2)}) collective-permute-start(bf16[512,1024]{1,0:T(8,128)(2,1)S(1)} %get-tuple-element.42), channel_id=1, source_target_pairs={{0,4},{4,0},{16,20},{20,16},{32,36},{36,32},{48,52},{52,48},{8,12}... | collective-permute-start | bytes 3145736 | tf_op jit(solution)/shard_map/ppermute | solution.py:36
  117.5 3.5 %slice-start.2 = ((s8[7602176]{0:T(1024)(128)(4,1)}), s8[4194304]{0:T(1024)(128)(4,1)S(1)}, s32[]{:S(2)}) async-start(s8[7602176]{0:T(1024)(128)(4,1)} %bitcast.169), calls=%async_computation.2 | async-start | bytes 8388608
  118.2 14.2 %collective-permute-start.23 = (bf16[128,3712]{1,0:T(8,128)(2,1)S(1)}, bf16[128,3712]{1,0:T(8,128)(2,1)S(1)}, u32[]{:S(2)}, u32[]{:S(2)}) collective-permute-start(bf16[128,3712]{1,0:T(8,128)(2,1)S(1)} %get-tuple-element.27), channel_id=1, source_target_pairs={{0,8},{4,20},{16,24},{20,36},{32,40},{36,52},{48,56},{52,4},{8,64}... | collective-permute-start | bytes 2850824 | tf_op jit(solution)/shard_map/ppermute | solution.py:32
  119.3 13.0 %collective-permute-start.24 = (bf16[128,3712]{1,0:T(8,128)(2,1)S(1)}, bf16[128,3712]{1,0:T(8,128)(2,1)S(1)}, u32[]{:S(2)}, u32[]{:S(2)}) collective-permute-start(bf16[128,3712]{1,0:T(8,128)(2,1)S(1)} %get-tuple-element.28), channel_id=1, source_target_pairs={{0,72},{4,52},{16,88},{20,4},{32,104},{36,20},{48,120},{52,36},{8,... | collective-permute-start | bytes 2850824 | tf_op jit(solution)/shard_map/ppermute | solution.py:32
  132.8 6.1 %collective-permute-start.27 = (bf16[32,3712]{1,0:T(8,128)(2,1)S(1)}, bf16[32,3712]{1,0:T(8,128)(2,1)S(1)}, u32[]{:S(2)}, u32[]{:S(2)}) collective-permute-start(bf16[32,3712]{1,0:T(8,128)(2,1)S(1)} %get-tuple-element.47), channel_id=1, source_target_pairs={{0,48},{4,76},{16,0},{20,92},{32,16},{36,108},{48,32},{52,124},{8,... | collective-permute-start | bytes 712712 | tf_op jit(solution)/shard_map/ppermute | solution.py:32
  135.8 9.0 %collective-permute-start.26 = (bf16[32,3712]{1,0:T(8,128)(2,1)S(1)}, bf16[32,3712]{1,0:T(8,128)(2,1)S(1)}, u32[]{:S(2)}, u32[]{:S(2)}) collective-permute-start(bf16[32,3712]{1,0:T(8,128)(2,1)S(1)} %get-tuple-element.48), channel_id=1, source_target_pairs={{0,16},{4,12},{16,32},{20,28},{32,48},{36,44},{48,0},{52,60},{8,24... | collective-permute-start | bytes 712712 | tf_op jit(solution)/shard_map/ppermute | solution.py:32
  135.8 9.0 %collective-permute-start.25 = (bf16[32,3712]{1,0:T(8,128)(2,1)S(1)}, bf16[32,3712]{1,0:T(8,128)(2,1)S(1)}, u32[]{:S(2)}, u32[]{:S(2)}) collective-permute-start(bf16[32,3712]{1,0:T(8,128)(2,1)S(1)} %get-tuple-element.46), channel_id=1, source_target_pairs={{0,32},{4,68},{16,48},{20,84},{32,0},{36,100},{48,16},{52,116},{8,... | collective-permute-start | bytes 712712 | tf_op jit(solution)/shard_map/ppermute | solution.py:32
  (2 other events, 6.3 us)
where the time goes:
time: 146 us
  starting transfers between devices  42.2 us (29%)
  waiting for transfers between devices  35.1 us (24%)
  matrix products  34.8 us (24%)
  local copies, waits for them, and re-layouts  16 us (11%)
  Pallas kernels  12.4 us (8%)
  other arithmetic  3.08 us (2%)
  between operations  2.01 us (1%)
    ppermute x14, starting transfers between devices, move(): return lax.ppermute(block, PLANE, plane_pairs(leg, way))  20.4 us
    ppermute x8, starting transfers between devices, swap(): lax.ppermute(block, PLANE, [(spot(z, y, c), spot(z, y, 1 - c)) for z in r...  12.7 us
    ppermute x2, waiting for transfers between devices, cross(): return lax.ppermute(block, ('col', 'depth'), pairs)  12.7 us
    dot_general x8, matrix products, shards(): product = jnp.dot(part, weight, preferred_element_type=f32)  12.6 us
    ppermute x4, waiting for transfers between devices, move(): return lax.ppermute(block, 'depth', [(i, (i + way) % 4) for i in range(4)])  12.3 us
    dot_general x1, matrix products, shards(): lax.dot_general(flat, beside, (((0,), (0,)), ((), ())), preferred_element...  10.5 us
    ppermute x14, waiting for transfers between devices, move(): return lax.ppermute(block, PLANE, plane_pairs(leg, way))  10 us
    dot_general x1, matrix products, shards(): rest = jnp.dot(rest, turned, preferred_element_type=f32)  9.53 us
  transfers between devices with their start and end apart: 28, of which 9 were waited for; matrix products, arithmetic and copies ran while one was open for 35% of the time, Pallas kernels for 8%

commit v1 on v0

--- a/solution.py
+++ b/solution.py
@@ -176,8 +176,6 @@
     near_mate = partner(near, core, 1)
     away = jnp.stack([pick(stack, slot(near)), pick(stack, slot(near_mate))], 0).astype(bf16)
     got = cross(away, 0)
-    turned = turn((w_up, held), away[0, :16, :128])
-    turned, got = tie(turned, got)
     send = (pick(stack, slot(mate)) + got[1].astype(f32)).astype(bf16)
     pre_act = pick(stack, slot(depth)) + got[0].astype(f32) + cross(send, 1).astype(f32)
 
@@ -188,6 +186,8 @@
     grad_own = (cotangent.reshape(pre_act.shape).astype(f32) * slope).astype(bf16)
 
     lower, upper = move(grad_own, "depth", 1), move(grad_own, "depth", -1)
+    turned = turn((w_up, held), grad_own[:16, :128])
+    turned, lower, upper = tie(turned, lower, upper)
     middle = count // 2
     opposite = jnp.concatenate(
         [move(lower[:middle], "depth", 1), move(upper[middle:], "depth", -1)], 0

time: 146 us -> 138 us (0.945)
  local copies, waits for them, and re-layouts: 16 us -> 6.95 us
    ppermute x2, waiting for transfers between devices: 12.7 us -> 19.8 us  [cross(): return lax.ppermute(block, ('col', 'depth'), pairs)]
    ppermute x4, waiting for transfers between devices: 12.3 us -> 6.29 us  [move(): return lax.ppermute(block, 'depth', [(i, (i + way) % 4) for i in range(4)])]
    dynamic_update_slice x4, local copies, waits for them, and re-layouts: 5.02 us -> 0.46 us  [shards(): lax.dynamic_update_slice(every, swap(part)[None, None], (1, (first + shif...]
    dynamic_update_slice x4, local copies, waits for them, and re-layouts: 3.07 us -> 0.48 us  [shards(): lax.dynamic_update_slice(every, part[None, None], (0, (second + shift) %...]
    unnamed x13 -> x7, local copies, waits for them, and re-layouts: 2 us -> 0.05 us
  transfers between devices with their start and end apart: 28 -> 28, of which waited for: 9 -> 9; matrix products, arithmetic and copies ran while one was open for 35% -> 32% of each run, Pallas kernels for 8% -> 9%
where the time goes in v1:
time: 138 us
  starting transfers between devices  42.2 us (31%)
  waiting for transfers between devices  36.2 us (26%)
  matrix products  35.2 us (26%)
  Pallas kernels  12.3 us (9%)
  local copies, waits for them, and re-layouts  6.95 us (5%)
  other arithmetic  3.02 us (2%)
  between operations  2.05 us (1%)
    ppermute x14, starting transfers between devices, move(): return lax.ppermute(block, PLANE, plane_pairs(leg, way))  20.4 us
    ppermute x2, waiting for transfers between devices, cross(): return lax.ppermute(block, ('col', 'depth'), pairs)  19.8 us
    ppermute x8, starting transfers between devices, swap(): lax.ppermute(block, PLANE, [(spot(z, y, c), spot(z, y, 1 - c)) for z in r...  13.8 us
    dot_general x8, matrix products, shards(): product = jnp.dot(part, weight, preferred_element_type=f32)  13 us
    dot_general x1, matrix products, shards(): lax.dot_general(flat, beside, (((0,), (0,)), ((), ())), preferred_element...  10.5 us
    ppermute x14, waiting for transfers between devices, move(): return lax.ppermute(block, PLANE, plane_pairs(leg, way))  10.1 us
    dot_general x1, matrix products, shards(): rest = jnp.dot(rest, turned, preferred_element_type=f32)  9.53 us
    pallas_call x1, Pallas kernels, turn(): pl.pallas_call(turn_block, grid=(len(matrices), count), in_specs=[pl.Bloc...  6.58 us
  transfers between devices with their start and end apart: 28, of which 9 were waited for; matrix products, arithmetic and copies ran while one was open for 32% of the time, Pallas kernels for 9%

profile of v1, /device:TPU:1, one launch (start us, length us, event | category | flops | bytes accessed | tf_op | source)
XLA Modules:
  0.0 138.0 jit_solution(1632942030924364311)
XLA Ops:
  0.6 1.5 %collective-permute-start.3 = (bf16[3712,1024]{1,0:T(8,128)(2,1)}, bf16[3712,1024]{1,0:T(8,128)(2,1)}, u32[]{:S(2)}, u32[]{:S(2)}) collective-permute-start(bf16[3712,1024]{1,0:T(8,128)(2,1)} %refs_0_.1), channel_id=1, source_target_pairs={{0,4},{4,0},{16,20},{20,16},{32,36},{36,32},{48,52},{52,48},{8,12}... | collective-permute-start | bytes 22806536 | tf_op jit(solution)/shard_map/ppermute | solution.py:36
  2.1 1.7 %collective-permute-start = (bf16[32,3712]{1,0:T(8,128)(2,1)}, bf16[32,3712]{1,0:T(8,128)(2,1)S(1)}, u32[]{:S(2)}, u32[]{:S(2)}) collective-permute-start(bf16[32,3712]{1,0:T(8,128)(2,1)} %param.3), channel_id=1, source_target_pairs={{0,16},{4,12},{16,32},{20,28},{32,48},{36,44},{48,0},{52,60},{8,24... | collective-permute-start | bytes 712712 | tf_op jit(solution)/shard_map/ppermute | solution.py:32
  3.9 3.3 %collective-permute-start.1 = (bf16[32,3712]{1,0:T(8,128)(2,1)}, bf16[32,3712]{1,0:T(8,128)(2,1)S(1)}, u32[]{:S(2)}, u32[]{:S(2)}) collective-permute-start(bf16[32,3712]{1,0:T(8,128)(2,1)} %param.3), channel_id=1, source_target_pairs={{0,32},{4,68},{16,48},{20,84},{32,0},{36,100},{48,16},{52,116},{8,... | collective-permute-start | bytes 712712 | tf_op jit(solution)/shard_map/ppermute | solution.py:32
  11.2 2.2 %collective-permute-done.1 = bf16[32,3712]{1,0:T(8,128)(2,1)S(1)} collective-permute-done((bf16[32,3712]{1,0:T(8,128)(2,1)}, bf16[32,3712]{1,0:T(8,128)(2,1)S(1)}, u32[]{:S(2)}, u32[]{:S(2)}) %collective-permute-start.1) | collective-permute-done | bytes 237600 | tf_op jit(solution)/shard_map/ppermute | solution.py:32
  13.5 1.4 collective-permute-start.4
  14.8 1.5 %collective-permute-start.5 = (bf16[128,3712]{1,0:T(8,128)(2,1)S(1)}, bf16[128,3712]{1,0:T(8,128)(2,1)S(1)}, u32[]{:S(2)}, u32[]{:S(2)}) collective-permute-start(bf16[128,3712]{1,0:T(8,128)(2,1)S(1)} %bitcast.155), channel_id=1, source_target_pairs={{0,72},{4,52},{16,88},{20,4},{32,104},{36,20},{48,120},{52,36},{8,... | collective-permute-start | bytes 2850824 | tf_op jit(solution)/shard_map/ppermute | solution.py:32
  16.4 1.5 %collective-permute-start.19 = (bf16[128,3712]{1,0:T(8,128)(2,1)S(1)}, bf16[128,3712]{1,0:T(8,128)(2,1)S(1)}, u32[]{:S(2)}, u32[]{:S(2)}) collective-permute-start(bf16[128,3712]{1,0:T(8,128)(2,1)S(1)} %bitcast.156), channel_id=1, source_target_pairs={{0,4},{4,0},{16,20},{20,16},{32,36},{36,32},{48,52},{52,48},{8,12}... | collective-permute-start | bytes 2850824 | tf_op jit(solution)/shard_map/ppermute | solution.py:36
  18.1 4.3 %fusion.13 = f32[4,128,1024]{2,1,0:T(8,128)S(1)} fusion(f32[4,128,1024]{2,1,0:T(8,128)S(1)} %broadcast.60.clone, s32[]{:T(128)S(6)} %select_n.424, bf16[128,3712]{1,0:T(8,128)(2,1)S(1)} %bitcast.157, bf16[3712,1024]{1,0:T(8,128)(2,1)} %refs_0_.1), kind=kOutput, calls=%fused_computation.34 | convolution fusion | flops 973078528 | bytes 9076740 | tf_op jit(solution)/shard_map/dot_general | solution.py:167
  23.4 5.8 %shard_map.58.refs_1_ = bf16[3712,1024]{1,0:T(8,128)(2,1)S(1)} custom-call(bf16[16,128]{1,0:T(8,128)(2,1)S(1)} %slice.84.after_ref, bf16[3712,1024]{1,0:T(8,128)(2,1)} %collective-permute-done.3.block_ref), custom_call_target="tpu_custom_call" | custom-call | bytes 15204352 | tf_op jit(solution)/shard_map/pallas_call | solution.py:116
  29.9 1.3 collective-permute-start.6
  31.3 1.4 collective-permute-start.7
  35.3 1.3 fusion.8
  36.8 1.3 fusion.11
  39.5 1.4 %collective-permute-start.22 = (bf16[128,3712]{1,0:T(8,128)(2,1)S(1)}, bf16[128,3712]{1,0:T(8,128)(2,1)S(1)}, u32[]{:S(2)}, u32[]{:S(2)}) collective-permute-start(bf16[128,3712]{1,0:T(8,128)(2,1)S(1)} %constant_dynamic-update-slice_fusion.1), channel_id=1, source_target_pairs={{0,4},{4,0},{16,20},{20,16},{32,36},{36,32},{48,52},{52,48},{8,12}... | collective-permute-start | bytes 2850824 | tf_op jit(solution)/shard_map/ppermute | solution.py:36
  43.9 2.6 %collective-permute-start.8 = (bf16[2,128,2048]{2,1,0:T(8,128)(2,1)S(1)}, bf16[2,128,2048]{2,1,0:T(8,128)(2,1)S(1)}, u32[]{:S(2)}, u32[]{:S(2)}) collective-permute-start(bf16[2,128,2048]{2,1,0:T(8,128)(2,1)S(1)} %pad_maximum_fusion.1), channel_id=1, source_target_pairs={{0,1},{1,0},{2,3},{3,2},{4,7},{5,6},{6,5},{7,4},{8,9},{9,8},{10,11... | collective-permute-start | bytes 3145736 | tf_op jit(solution)/shard_map/ppermute | solution.py:71
  46.9 11.9 %collective-permute-done.8 = bf16[2,128,2048]{2,1,0:T(8,128)(2,1)S(1)} collective-permute-done((bf16[2,128,2048]{2,1,0:T(8,128)(2,1)S(1)}, bf16[2,128,2048]{2,1,0:T(8,128)(2,1)S(1)}, u32[]{:S(2)}, u32[]{:S(2)}) %collective-permute-start.8) | collective-permute-done | bytes 1048608 | tf_op jit(solution)/shard_map/ppermute | solution.py:71
  59.5 7.9 %collective-permute-done.9 = bf16[128,2048]{1,0:T(8,128)(2,1)S(1)} collective-permute-done((bf16[128,2048]{1,0:T(8,128)(2,1)S(1)}, bf16[128,2048]{1,0:T(8,128)(2,1)S(1)}, u32[]{:S(2)}, u32[]{:S(2)}) %collective-permute-start.9) | collective-permute-done | bytes 524320 | tf_op jit(solution)/shard_map/ppermute | solution.py:71
  68.4 2.4 %collective-permute-start.13 = (bf16[128,2048]{1,0:T(8,128)(2,1)S(1)}, bf16[128,2048]{1,0:T(8,128)(2,1)S(1)}, u32[]{:S(2)}, u32[]{:S(2)}) collective-permute-start(bf16[128,2048]{1,0:T(8,128)(2,1)S(1)} %get-tuple-element.35), channel_id=1, source_target_pairs={{0,3},{1,0},{2,1},{3,2},{4,7},{5,4},{6,5},{7,6},{8,11},{9,8},{10,9... | collective-permute-start | bytes 1572872 | tf_op jit(solution)/shard_map/ppermute | solution.py:31
  71.0 2.9 %collective-permute-start.10 = (bf16[2,2,32,1024]{3,2,1,0:T(8,128)(2,1)S(1)}, bf16[2,2,32,1024]{3,2,1,0:T(8,128)(2,1)S(1)}, u32[]{:S(2)}, u32[]{:S(2)}) collective-permute-start(bf16[2,2,32,1024]{3,2,1,0:T(8,128)(2,1)S(1)} %bitcast_select_fusion), channel_id=1, source_target_pairs={{0,4},{4,0},{16,20},{20,16},{32,36},{36,32},{48,52},{52,48},{8,12}... | collective-permute-start | bytes 786440 | tf_op jit(solution)/shard_map/ppermute | solution.py:36
  73.9 6.6 %shard_map.59 = bf16[2048,3712]{1,0:T(8,128)(2,1)S(1)} custom-call(bf16[16,128]{1,0:T(8,128)(2,1)S(1)} %slice.89.after_ref, bf16[3712,1024]{1,0:T(8,128)(2,1)S(1)} %bitcast.147, bf16[3712,1024]{1,0:T(8,128)(2,1)S(1)} %shard_map.58.refs_1_), custom_call_target="tpu_custom_call" | custom-call | bytes 30408704 | tf_op jit(solution)/shard_map/pallas_call | solution.py:95
  80.9 2.3 %collective-permute-start.15 = (bf16[64,2048]{1,0:T(8,128)(2,1)S(1)}, bf16[64,2048]{1,0:T(8,128)(2,1)S(1)}, u32[]{:S(2)}, u32[]{:S(2)}) collective-permute-start(bf16[64,2048]{1,0:T(8,128)(2,1)S(1)} %slice.74), channel_id=1, source_target_pairs={{0,3},{1,0},{2,1},{3,2},{4,7},{5,4},{6,5},{7,6},{8,11},{9,8},{10,9... | collective-permute-start | bytes 786440 | tf_op jit(solution)/shard_map/ppermute | solution.py:31
  83.4 3.1 %collective-permute-done.15 = bf16[64,2048]{1,0:T(8,128)(2,1)S(1)} collective-permute-done((bf16[64,2048]{1,0:T(8,128)(2,1)S(1)}, bf16[64,2048]{1,0:T(8,128)(2,1)S(1)}, u32[]{:S(2)}, u32[]{:S(2)}) %collective-permute-start.15) | collective-permute-done | bytes 262176 | tf_op jit(solution)/shard_map/ppermute | solution.py:31
  86.5 3.2 %collective-permute-done.14 = bf16[64,2048]{1,0:T(8,128)(2,1)S(1)} collective-permute-done((bf16[64,2048]{1,0:T(8,128)(2,1)S(1)}, bf16[64,2048]{1,0:T(8,128)(2,1)S(1)}, u32[]{:S(2)}, u32[]{:S(2)}) %collective-permute-start.14) | collective-permute-done | bytes 262176 | tf_op jit(solution)/shard_map/ppermute | solution.py:31
  89.8 2.2 %convolution_convert_fusion.1 = bf16[128,3712]{1,0:T(8,128)(2,1)S(1)} fusion(bf16[128,2048]{1,0:T(8,128)(2,1)S(1)} %bitcast.172, bf16[2048,3712]{1,0:T(8,128)(2,1)S(1)} %shard_map.59), kind=kOutput, calls=%fused_computation.9 | convolution fusion | flops 1946632192 | bytes 16678912 | tf_op jit(solution)/shard_map/dot_general | solution.py:206
  92.2 2.0 %collective-permute-start.17 = (bf16[64,3712]{1,0:T(8,128)(2,1)S(1)}, bf16[64,3712]{1,0:T(8,128)(2,1)S(1)}, u32[]{:S(2)}, u32[]{:S(2)}) collective-permute-start(bf16[64,3712]{1,0:T(8,128)(2,1)S(1)} %get-tuple-element.53), channel_id=1, source_target_pairs={{0,72},{4,52},{16,88},{20,4},{32,104},{36,20},{48,120},{52,36},{8,... | collective-permute-start | bytes 1425416 | tf_op jit(solution)/shard_map/ppermute | solution.py:32
  94.6 5.5 %collective-permute-start.18 = (bf16[512,1024]{1,0:T(8,128)(2,1)S(1)}, bf16[512,1024]{1,0:T(8,128)(2,1)S(1)}, u32[]{:S(2)}, u32[]{:S(2)}) collective-permute-start(bf16[512,1024]{1,0:T(8,128)(2,1)S(1)} %get-tuple-element.44), channel_id=1, source_target_pairs={{0,4},{4,0},{16,20},{20,16},{32,36},{36,32},{48,52},{52,48},{8,12}... | collective-permute-start | bytes 3145736 | tf_op jit(solution)/shard_map/ppermute | solution.py:36
  100.2 9.5 %fusion.46 = (bf16[384,3712]{1,0:T(8,128)(2,1)S(1)}, f32[384,3712]{1,0:T(8,128)S(1)}) fusion(bf16[2048,3712]{1,0:T(8,128)(2,1)} %copy-done, bf16[128,2048]{1,0:T(8,128)(2,1)S(1)} %bitcast.174, bf16[128,2048]{1,0:T(8,128)(2,1)S(1)} %bitcast.175, bf16[128,2048]{1,0:T(8,128)(2,1)S(1)} %bitcast.173), kind=kOutput, calls=%fused_computation.109 | convolution fusion | flops 5844615168 | bytes 25329664 | tf_op jit(solution)/shard_map/dot_general | solution.py:210
  110.5 1.4 %collective-permute-start.23 = (bf16[128,3712]{1,0:T(8,128)(2,1)S(1)}, bf16[128,3712]{1,0:T(8,128)(2,1)S(1)}, u32[]{:S(2)}, u32[]{:S(2)}) collective-permute-start(bf16[128,3712]{1,0:T(8,128)(2,1)S(1)} %get-tuple-element.29), channel_id=1, source_target_pairs={{0,8},{4,20},{16,24},{20,36},{32,40},{36,52},{48,56},{52,4},{8,64}... | collective-permute-start | bytes 2850824 | tf_op jit(solution)/shard_map/ppermute | solution.py:32
  111.9 1.4 collective-permute-start.24
  113.2 10.5 %convolution_convert_fusion = bf16[3712,1024]{1,0:T(8,128)(2,1)} fusion(bf16[1024,3712]{1,0:T(8,128)(2,1)S(1)} %bitcast.167, bf16[1024,1024]{1,0:T(8,128)(2,1)S(1)} %pad_maximum_fusion), kind=kOutput, calls=%fused_computation | convolution fusion | flops 7788429312 | bytes 17301504 | tf_op jit(solution)/shard_map/dot_general | solution.py:220
  125.2 3.0 %collective-permute-start.27 = (bf16[32,3712]{1,0:T(8,128)(2,1)S(1)}, bf16[32,3712]{1,0:T(8,128)(2,1)S(1)}, u32[]{:S(2)}, u32[]{:S(2)}) collective-permute-start(bf16[32,3712]{1,0:T(8,128)(2,1)S(1)} %get-tuple-element.49), channel_id=1, source_target_pairs={{0,48},{4,76},{16,0},{20,92},{32,16},{36,108},{48,32},{52,124},{8,... | collective-permute-start | bytes 712712 | tf_op jit(solution)/shard_map/ppermute | solution.py:32
  131.3 6.0 %collective-permute-done.26 = bf16[32,3712]{1,0:T(8,128)(2,1)S(1)} collective-permute-done((bf16[32,3712]{1,0:T(8,128)(2,1)S(1)}, bf16[32,3712]{1,0:T(8,128)(2,1)S(1)}, u32[]{:S(2)}, u32[]{:S(2)}) %collective-permute-start.26) | collective-permute-done | bytes 237600 | tf_op jit(solution)/shard_map/ppermute | solution.py:32
  (100 shorter events, 21.8 us)
Async XLA Ops:
  0.6 22.8 %collective-permute-start.3 = (bf16[3712,1024]{1,0:T(8,128)(2,1)}, bf16[3712,1024]{1,0:T(8,128)(2,1)}, u32[]{:S(2)}, u32[]{:S(2)}) collective-permute-start(bf16[3712,1024]{1,0:T(8,128)(2,1)} %refs_0_.1), channel_id=1, source_target_pairs={{0,4},{4,0},{16,20},{20,16},{32,36},{36,32},{48,52},{52,48},{8,12}... | collective-permute-start | bytes 22806536 | tf_op jit(solution)/shard_map/ppermute | solution.py:36
  2.1 9.0 %collective-permute-start = (bf16[32,3712]{1,0:T(8,128)(2,1)}, bf16[32,3712]{1,0:T(8,128)(2,1)S(1)}, u32[]{:S(2)}, u32[]{:S(2)}) collective-permute-start(bf16[32,3712]{1,0:T(8,128)(2,1)} %param.3), channel_id=1, source_target_pairs={{0,16},{4,12},{16,32},{20,28},{32,48},{36,44},{48,0},{52,60},{8,24... | collective-permute-start | bytes 712712 | tf_op jit(solution)/shard_map/ppermute | solution.py:32
  3.9 9.6 %collective-permute-start.1 = (bf16[32,3712]{1,0:T(8,128)(2,1)}, bf16[32,3712]{1,0:T(8,128)(2,1)S(1)}, u32[]{:S(2)}, u32[]{:S(2)}) collective-permute-start(bf16[32,3712]{1,0:T(8,128)(2,1)} %param.3), channel_id=1, source_target_pairs={{0,32},{4,68},{16,48},{20,84},{32,0},{36,100},{48,16},{52,116},{8,... | collective-permute-start | bytes 712712 | tf_op jit(solution)/shard_map/ppermute | solution.py:32
  7.2 6.3 %collective-permute-start.2 = (bf16[32,3712]{1,0:T(8,128)(2,1)}, bf16[32,3712]{1,0:T(8,128)(2,1)S(1)}, u32[]{:S(2)}, u32[]{:S(2)}) collective-permute-start(bf16[32,3712]{1,0:T(8,128)(2,1)} %param.3), channel_id=1, source_target_pairs={{0,48},{4,76},{16,0},{20,92},{32,16},{36,108},{48,32},{52,124},{8,... | collective-permute-start | bytes 712712 | tf_op jit(solution)/shard_map/ppermute | solution.py:32
  9.0 14.2 %collective-permute-start.11 = (bf16[2,2,32,1024]{3,2,1,0:T(8,128)(2,1)S(1)}, bf16[2,2,32,1024]{3,2,1,0:T(8,128)(2,1)S(1)}, u32[]{:S(2)}, u32[]{:S(2)}) collective-permute-start(bf16[2,2,32,1024]{3,2,1,0:T(8,128)(2,1)S(1)} %get-tuple-element.58), channel_id=1, source_target_pairs={{0,4},{4,0},{16,20},{20,16},{32,36},{36,32},{48,52},{52,48},{8,12}... | collective-permute-start | bytes 786440 | tf_op jit(solution)/shard_map/ppermute | solution.py:36
  13.5 15.7 %collective-permute-start.4 = (bf16[128,3712]{1,0:T(8,128)(2,1)S(1)}, bf16[128,3712]{1,0:T(8,128)(2,1)S(1)}, u32[]{:S(2)}, u32[]{:S(2)}) collective-permute-start(bf16[128,3712]{1,0:T(8,128)(2,1)S(1)} %bitcast.154), channel_id=1, source_target_pairs={{0,8},{4,20},{16,24},{20,36},{32,40},{36,52},{48,56},{52,4},{8,64}... | collective-permute-start | bytes 2850824 | tf_op jit(solution)/shard_map/ppermute | solution.py:32
  14.8 14.3 %collective-permute-start.5 = (bf16[128,3712]{1,0:T(8,128)(2,1)S(1)}, bf16[128,3712]{1,0:T(8,128)(2,1)S(1)}, u32[]{:S(2)}, u32[]{:S(2)}) collective-permute-start(bf16[128,3712]{1,0:T(8,128)(2,1)S(1)} %bitcast.155), channel_id=1, source_target_pairs={{0,72},{4,52},{16,88},{20,4},{32,104},{36,20},{48,120},{52,36},{8,... | collective-permute-start | bytes 2850824 | tf_op jit(solution)/shard_map/ppermute | solution.py:32
  16.4 6.9 %collective-permute-start.19 = (bf16[128,3712]{1,0:T(8,128)(2,1)S(1)}, bf16[128,3712]{1,0:T(8,128)(2,1)S(1)}, u32[]{:S(2)}, u32[]{:S(2)}) collective-permute-start(bf16[128,3712]{1,0:T(8,128)(2,1)S(1)} %bitcast.156), channel_id=1, source_target_pairs={{0,4},{4,0},{16,20},{20,16},{32,36},{36,32},{48,52},{52,48},{8,12}... | collective-permute-start | bytes 2850824 | tf_op jit(solution)/shard_map/ppermute | solution.py:36
  23.2 9.4 %slice-start = ((s8[7602176]{0:T(1024)(128)(4,1)}), s8[4194304]{0:T(1024)(128)(4,1)S(1)}, s32[]{:S(2)}) async-start(s8[7602176]{0:T(1024)(128)(4,1)} %bitcast.146), calls=%async_computation | async-start | bytes 8388608
  23.4 9.2 %slice-start.1 = ((s8[7602176]{0:T(1024)(128)(4,1)}), s8[3407872]{0:T(1024)(128)(4,1)S(1)}, s32[]{:S(2)}) async-start(s8[7602176]{0:T(1024)(128)(4,1)} %bitcast.146), calls=%async_computation.1 | async-start | bytes 6815744
  29.2 17.2 %collective-permute-start.20 = (bf16[128,3712]{1,0:T(8,128)(2,1)S(1)}, bf16[128,3712]{1,0:T(8,128)(2,1)S(1)}, u32[]{:S(2)}, u32[]{:S(2)}) collective-permute-start(bf16[128,3712]{1,0:T(8,128)(2,1)S(1)} %collective-permute-done.4), channel_id=1, source_target_pairs={{0,4},{4,0},{16,20},{20,16},{32,36},{36,32},{48,52},{52,48},{8,12}... | collective-permute-start | bytes 2850824 | tf_op jit(solution)/shard_map/ppermute | solution.py:36
  29.7 17.0 %collective-permute-start.21 = (bf16[128,3712]{1,0:T(8,128)(2,1)S(1)}, bf16[128,3712]{1,0:T(8,128)(2,1)S(1)}, u32[]{:S(2)}, u32[]{:S(2)}) collective-permute-start(bf16[128,3712]{1,0:T(8,128)(2,1)S(1)} %collective-permute-done.5), channel_id=1, source_target_pairs={{0,4},{4,0},{16,20},{20,16},{32,36},{36,32},{48,52},{52,48},{8,12}... | collective-permute-start | bytes 2850824 | tf_op jit(solution)/shard_map/ppermute | solution.py:36
  29.9 9.4 %collective-permute-start.6 = (bf16[64,3712]{1,0:T(8,128)(2,1)S(1)}, bf16[64,3712]{1,0:T(8,128)(2,1)S(1)}, u32[]{:S(2)}, u32[]{:S(2)}) collective-permute-start(bf16[64,3712]{1,0:T(8,128)(2,1)S(1)} %slice.66), channel_id=1, source_target_pairs={{0,8},{4,20},{16,24},{20,36},{32,40},{36,52},{48,56},{52,4},{8,64}... | collective-permute-start | bytes 1425416 | tf_op jit(solution)/shard_map/ppermute | solution.py:32
  31.3 8.1 %collective-permute-start.7 = (bf16[64,3712]{1,0:T(8,128)(2,1)S(1)}, bf16[64,3712]{1,0:T(8,128)(2,1)S(1)}, u32[]{:S(2)}, u32[]{:S(2)}) collective-permute-start(bf16[64,3712]{1,0:T(8,128)(2,1)S(1)} %slice.67), channel_id=1, source_target_pairs={{0,72},{4,52},{16,88},{20,4},{32,104},{36,20},{48,120},{52,36},{8,... | collective-permute-start | bytes 1425416 | tf_op jit(solution)/shard_map/ppermute | solution.py:32
  39.5 19.9 %collective-permute-start.22 = (bf16[128,3712]{1,0:T(8,128)(2,1)S(1)}, bf16[128,3712]{1,0:T(8,128)(2,1)S(1)}, u32[]{:S(2)}, u32[]{:S(2)}) collective-permute-start(bf16[128,3712]{1,0:T(8,128)(2,1)S(1)} %constant_dynamic-update-slice_fusion.1), channel_id=1, source_target_pairs={{0,4},{4,0},{16,20},{20,16},{32,36},{36,32},{48,52},{52,48},{8,12}... | collective-permute-start | bytes 2850824 | tf_op jit(solution)/shard_map/ppermute | solution.py:36
  43.9 14.9 %collective-permute-start.8 = (bf16[2,128,2048]{2,1,0:T(8,128)(2,1)S(1)}, bf16[2,128,2048]{2,1,0:T(8,128)(2,1)S(1)}, u32[]{:S(2)}, u32[]{:S(2)}) collective-permute-start(bf16[2,128,2048]{2,1,0:T(8,128)(2,1)S(1)} %pad_maximum_fusion.1), channel_id=1, source_target_pairs={{0,1},{1,0},{2,3},{3,2},{4,7},{5,6},{6,5},{7,4},{8,9},{9,8},{10,11... | collective-permute-start | bytes 3145736 | tf_op jit(solution)/shard_map/ppermute | solution.py:71
  59.0 8.4 %collective-permute-start.9 = (bf16[128,2048]{1,0:T(8,128)(2,1)S(1)}, bf16[128,2048]{1,0:T(8,128)(2,1)S(1)}, u32[]{:S(2)}, u32[]{:S(2)}) collective-permute-start(bf16[128,2048]{1,0:T(8,128)(2,1)S(1)} %fusion.33), channel_id=1, source_target_pairs={{0,3},{1,2},{2,1},{3,0},{4,5},{5,4},{6,7},{7,6},{8,11},{9,10},{10,... | collective-permute-start | bytes 1572872 | tf_op jit(solution)/shard_map/ppermute | solution.py:71
  68.0 12.8 %collective-permute-start.12 = (bf16[128,2048]{1,0:T(8,128)(2,1)S(1)}, bf16[128,2048]{1,0:T(8,128)(2,1)S(1)}, u32[]{:S(2)}, u32[]{:S(2)}) collective-permute-start(bf16[128,2048]{1,0:T(8,128)(2,1)S(1)} %get-tuple-element.35), channel_id=1, source_target_pairs={{0,1},{1,2},{2,3},{3,0},{4,5},{5,6},{6,7},{7,4},{8,9},{9,10},{10,1... | collective-permute-start | bytes 1572872 | tf_op jit(solution)/shard_map/ppermute | solution.py:31
  68.4 12.5 %collective-permute-start.13 = (bf16[128,2048]{1,0:T(8,128)(2,1)S(1)}, bf16[128,2048]{1,0:T(8,128)(2,1)S(1)}, u32[]{:S(2)}, u32[]{:S(2)}) collective-permute-start(bf16[128,2048]{1,0:T(8,128)(2,1)S(1)} %get-tuple-element.35), channel_id=1, source_target_pairs={{0,3},{1,0},{2,1},{3,2},{4,7},{5,4},{6,5},{7,6},{8,11},{9,8},{10,9... | collective-permute-start | bytes 1572872 | tf_op jit(solution)/shard_map/ppermute | solution.py:31
  71.0 58.4 %collective-permute-start.10 = (bf16[2,2,32,1024]{3,2,1,0:T(8,128)(2,1)S(1)}, bf16[2,2,32,1024]{3,2,1,0:T(8,128)(2,1)S(1)}, u32[]{:S(2)}, u32[]{:S(2)}) collective-permute-start(bf16[2,2,32,1024]{3,2,1,0:T(8,128)(2,1)S(1)} %bitcast_select_fusion), channel_id=1, source_target_pairs={{0,4},{4,0},{16,20},{20,16},{32,36},{36,32},{48,52},{52,48},{8,12}... | collective-permute-start | bytes 786440 | tf_op jit(solution)/shard_map/ppermute | solution.py:36
  80.5 11.6 %copy-start = (bf16[2048,3712]{1,0:T(8,128)(2,1)}, bf16[2048,3712]{1,0:T(8,128)(2,1)S(1)}, u32[]{:S(2)}) copy-start(bf16[2048,3712]{1,0:T(8,128)(2,1)S(1)} %shard_map.59) | copy-start | bytes 45613060
  80.9 5.6 %collective-permute-start.15 = (bf16[64,2048]{1,0:T(8,128)(2,1)S(1)}, bf16[64,2048]{1,0:T(8,128)(2,1)S(1)}, u32[]{:S(2)}, u32[]{:S(2)}) collective-permute-start(bf16[64,2048]{1,0:T(8,128)(2,1)S(1)} %slice.74), channel_id=1, source_target_pairs={{0,3},{1,0},{2,1},{3,2},{4,7},{5,4},{6,5},{7,6},{8,11},{9,8},{10,9... | collective-permute-start | bytes 786440 | tf_op jit(solution)/shard_map/ppermute | solution.py:31
  83.2 6.5 %collective-permute-start.14 = (bf16[64,2048]{1,0:T(8,128)(2,1)S(1)}, bf16[64,2048]{1,0:T(8,128)(2,1)S(1)}, u32[]{:S(2)}, u32[]{:S(2)}) collective-permute-start(bf16[64,2048]{1,0:T(8,128)(2,1)S(1)} %slice.73), channel_id=1, source_target_pairs={{0,1},{1,2},{2,3},{3,0},{4,5},{5,6},{6,7},{7,4},{8,9},{9,10},{10,1... | collective-permute-start | bytes 786440 | tf_op jit(solution)/shard_map/ppermute | solution.py:31
  92.2 17.8 %collective-permute-start.17 = (bf16[64,3712]{1,0:T(8,128)(2,1)S(1)}, bf16[64,3712]{1,0:T(8,128)(2,1)S(1)}, u32[]{:S(2)}, u32[]{:S(2)}) collective-permute-start(bf16[64,3712]{1,0:T(8,128)(2,1)S(1)} %get-tuple-element.53), channel_id=1, source_target_pairs={{0,72},{4,52},{16,88},{20,4},{32,104},{36,20},{48,120},{52,36},{8,... | collective-permute-start | bytes 1425416 | tf_op jit(solution)/shard_map/ppermute | solution.py:32
  94.2 15.8 %collective-permute-start.16 = (bf16[64,3712]{1,0:T(8,128)(2,1)S(1)}, bf16[64,3712]{1,0:T(8,128)(2,1)S(1)}, u32[]{:S(2)}, u32[]{:S(2)}) collective-permute-start(bf16[64,3712]{1,0:T(8,128)(2,1)S(1)} %get-tuple-element.54), channel_id=1, source_target_pairs={{0,8},{4,20},{16,24},{20,36},{32,40},{36,52},{48,56},{52,4},{8,64}... | collective-permute-start | bytes 1425416 | tf_op jit(solution)/shard_map/ppermute | solution.py:32
  94.6 15.7 %collective-permute-start.18 = (bf16[512,1024]{1,0:T(8,128)(2,1)S(1)}, bf16[512,1024]{1,0:T(8,128)(2,1)S(1)}, u32[]{:S(2)}, u32[]{:S(2)}) collective-permute-start(bf16[512,1024]{1,0:T(8,128)(2,1)S(1)} %get-tuple-element.44), channel_id=1, source_target_pairs={{0,4},{4,0},{16,20},{20,16},{32,36},{36,32},{48,52},{52,48},{8,12}... | collective-permute-start | bytes 3145736 | tf_op jit(solution)/shard_map/ppermute | solution.py:36
  110.5 14.2 %collective-permute-start.23 = (bf16[128,3712]{1,0:T(8,128)(2,1)S(1)}, bf16[128,3712]{1,0:T(8,128)(2,1)S(1)}, u32[]{:S(2)}, u32[]{:S(2)}) collective-permute-start(bf16[128,3712]{1,0:T(8,128)(2,1)S(1)} %get-tuple-element.29), channel_id=1, source_target_pairs={{0,8},{4,20},{16,24},{20,36},{32,40},{36,52},{48,56},{52,4},{8,64}... | collective-permute-start | bytes 2850824 | tf_op jit(solution)/shard_map/ppermute | solution.py:32
  111.9 12.9 %collective-permute-start.24 = (bf16[128,3712]{1,0:T(8,128)(2,1)S(1)}, bf16[128,3712]{1,0:T(8,128)(2,1)S(1)}, u32[]{:S(2)}, u32[]{:S(2)}) collective-permute-start(bf16[128,3712]{1,0:T(8,128)(2,1)S(1)} %get-tuple-element.30), channel_id=1, source_target_pairs={{0,72},{4,52},{16,88},{20,4},{32,104},{36,20},{48,120},{52,36},{8,... | collective-permute-start | bytes 2850824 | tf_op jit(solution)/shard_map/ppermute | solution.py:32
  125.2 6.1 %collective-permute-start.27 = (bf16[32,3712]{1,0:T(8,128)(2,1)S(1)}, bf16[32,3712]{1,0:T(8,128)(2,1)S(1)}, u32[]{:S(2)}, u32[]{:S(2)}) collective-permute-start(bf16[32,3712]{1,0:T(8,128)(2,1)S(1)} %get-tuple-element.49), channel_id=1, source_target_pairs={{0,48},{4,76},{16,0},{20,92},{32,16},{36,108},{48,32},{52,124},{8,... | collective-permute-start | bytes 712712 | tf_op jit(solution)/shard_map/ppermute | solution.py:32
  128.2 9.0 %collective-permute-start.26 = (bf16[32,3712]{1,0:T(8,128)(2,1)S(1)}, bf16[32,3712]{1,0:T(8,128)(2,1)S(1)}, u32[]{:S(2)}, u32[]{:S(2)}) collective-permute-start(bf16[32,3712]{1,0:T(8,128)(2,1)S(1)} %get-tuple-element.50), channel_id=1, source_target_pairs={{0,16},{4,12},{16,32},{20,28},{32,48},{36,44},{48,0},{52,60},{8,24... | collective-permute-start | bytes 712712 | tf_op jit(solution)/shard_map/ppermute | solution.py:32
  128.2 9.0 %collective-permute-start.25 = (bf16[32,3712]{1,0:T(8,128)(2,1)S(1)}, bf16[32,3712]{1,0:T(8,128)(2,1)S(1)}, u32[]{:S(2)}, u32[]{:S(2)}) collective-permute-start(bf16[32,3712]{1,0:T(8,128)(2,1)S(1)} %get-tuple-element.48), channel_id=1, source_target_pairs={{0,32},{4,68},{16,48},{20,84},{32,0},{36,100},{48,16},{52,116},{8,... | collective-permute-start | bytes 712712 | tf_op jit(solution)/shard_map/ppermute | solution.py:32

commit v2 on v1

--- a/solution.py
+++ b/solution.py
@@ -50,7 +50,7 @@
 
 def gather_near(block, leg, at):
     whole = jnp.zeros((4,) + block.shape, block.dtype)
-    for shift in (0, 1, 2, 3):
+    for shift in (0, 2, 3, 1):
         part = move(block, leg, shift) if shift else block
         whole = place(whole, part, at + 4 - shift)
     return whole
@@ -58,7 +58,7 @@
 
 def scatter_near(stack, leg, at):
     total = pick(stack, at)
-    for shift in (2, 1, 3):
+    for shift in (1, 3, 2):
         total += move(pick(stack, (at + shift) % 4).astype(bf16), leg, shift).astype(f32)
     return total
 

time: 138 us -> 136 us (0.986)
    ppermute x14, starting transfers between devices: 20.4 us -> 18.5 us  [move(): return lax.ppermute(block, PLANE, plane_pairs(leg, way))]
  transfers between devices with their start and end apart: 28 -> 28, of which waited for: 9 -> 8; matrix products, arithmetic and copies ran while one was open for 32% -> 32% of each run, Pallas kernels for 9% -> 9%
where the time goes in v2:
time: 136 us
  starting transfers between devices  41.6 us (31%)
  matrix products  35.2 us (26%)
  waiting for transfers between devices  35.1 us (26%)
  Pallas kernels  12.3 us (9%)
  local copies, waits for them, and re-layouts  6.96 us (5%)
  other arithmetic  3.02 us (2%)
  between operations  2.06 us (2%)
    ppermute x2, waiting for transfers between devices, cross(): return lax.ppermute(block, ('col', 'depth'), pairs)  19.8 us
    ppermute x14, starting transfers between devices, move(): return lax.ppermute(block, PLANE, plane_pairs(leg, way))  18.5 us
    ppermute x8, starting transfers between devices, swap(): lax.ppermute(block, PLANE, [(spot(z, y, c), spot(z, y, 1 - c)) for z in r...  15.1 us
    dot_general x8, matrix products, shards(): product = jnp.dot(part, weight, preferred_element_type=f32)  13 us
    dot_general x1, matrix products, shards(): lax.dot_general(flat, beside, (((0,), (0,)), ((), ())), preferred_element...  10.5 us
    dot_general x1, matrix products, shards(): rest = jnp.dot(rest, turned, preferred_element_type=f32)  9.53 us
    ppermute x14, waiting for transfers between devices, move(): return lax.ppermute(block, PLANE, plane_pairs(leg, way))  8.99 us
    pallas_call x1, Pallas kernels, turn(): pl.pallas_call(turn_block, grid=(len(matrices), count), in_specs=[pl.Bloc...  6.58 us
  transfers between devices with their start and end apart: 28, of which 8 were waited for; matrix products, arithmetic and copies ran while one was open for 32% of the time, Pallas kernels for 9%

profile of v2, /device:TPU:1, one launch (start us, length us, event | category | flops | bytes accessed | tf_op | source)
XLA Modules:
  0.0 136.3 jit_solution(7256039687727611438)
XLA Ops:
  0.6 1.5 %collective-permute-start.3 = (bf16[3712,1024]{1,0:T(8,128)(2,1)}, bf16[3712,1024]{1,0:T(8,128)(2,1)}, u32[]{:S(2)}, u32[]{:S(2)}) collective-permute-start(bf16[3712,1024]{1,0:T(8,128)(2,1)} %refs_0_.1), channel_id=1, source_target_pairs={{0,4},{4,0},{16,20},{20,16},{32,36},{36,32},{48,52},{52,48},{8,12}... | collective-permute-start | bytes 22806536 | tf_op jit(solution)/shard_map/ppermute | solution.py:36
  2.1 3.7 %collective-permute-start = (bf16[32,3712]{1,0:T(8,128)(2,1)}, bf16[32,3712]{1,0:T(8,128)(2,1)S(1)}, u32[]{:S(2)}, u32[]{:S(2)}) collective-permute-start(bf16[32,3712]{1,0:T(8,128)(2,1)} %param.3), channel_id=1, source_target_pairs={{0,32},{4,68},{16,48},{20,84},{32,0},{36,100},{48,16},{52,116},{8,... | collective-permute-start | bytes 712712 | tf_op jit(solution)/shard_map/ppermute | solution.py:32
  10.6 2.6 %collective-permute-done.1 = bf16[32,3712]{1,0:T(8,128)(2,1)S(1)} collective-permute-done((bf16[32,3712]{1,0:T(8,128)(2,1)}, bf16[32,3712]{1,0:T(8,128)(2,1)S(1)}, u32[]{:S(2)}, u32[]{:S(2)}) %collective-permute-start.1) | collective-permute-done | bytes 237600 | tf_op jit(solution)/shard_map/ppermute | solution.py:32
  14.3 1.7 %collective-permute-start.5 = (bf16[128,3712]{1,0:T(8,128)(2,1)S(1)}, bf16[128,3712]{1,0:T(8,128)(2,1)S(1)}, u32[]{:S(2)}, u32[]{:S(2)}) collective-permute-start(bf16[128,3712]{1,0:T(8,128)(2,1)S(1)} %bitcast.155), channel_id=1, source_target_pairs={{0,72},{4,52},{16,88},{20,4},{32,104},{36,20},{48,120},{52,36},{8,... | collective-permute-start | bytes 2850824 | tf_op jit(solution)/shard_map/ppermute | solution.py:32
  16.0 2.3 %collective-permute-start.19 = (bf16[128,3712]{1,0:T(8,128)(2,1)S(1)}, bf16[128,3712]{1,0:T(8,128)(2,1)S(1)}, u32[]{:S(2)}, u32[]{:S(2)}) collective-permute-start(bf16[128,3712]{1,0:T(8,128)(2,1)S(1)} %bitcast.156), channel_id=1, source_target_pairs={{0,4},{4,0},{16,20},{20,16},{32,36},{36,32},{48,52},{52,48},{8,12}... | collective-permute-start | bytes 2850824 | tf_op jit(solution)/shard_map/ppermute | solution.py:36
  18.6 4.3 %fusion.13 = f32[4,128,1024]{2,1,0:T(8,128)S(1)} fusion(f32[4,128,1024]{2,1,0:T(8,128)S(1)} %broadcast.60.clone, s32[]{:T(128)S(6)} %select_n.424, bf16[128,3712]{1,0:T(8,128)(2,1)S(1)} %bitcast.157, bf16[3712,1024]{1,0:T(8,128)(2,1)} %refs_0_.1), kind=kOutput, calls=%fused_computation.34 | convolution fusion | flops 973078528 | bytes 9076740 | tf_op jit(solution)/shard_map/dot_general | solution.py:167
  23.8 5.8 %shard_map.58.refs_1_ = bf16[3712,1024]{1,0:T(8,128)(2,1)S(1)} custom-call(bf16[16,128]{1,0:T(8,128)(2,1)S(1)} %slice.84.after_ref, bf16[3712,1024]{1,0:T(8,128)(2,1)} %collective-permute-done.3.block_ref), custom_call_target="tpu_custom_call" | custom-call | bytes 15204352 | tf_op jit(solution)/shard_map/pallas_call | solution.py:116
  30.4 2.7 %collective-permute-start.7 = (bf16[64,3712]{1,0:T(8,128)(2,1)S(1)}, bf16[64,3712]{1,0:T(8,128)(2,1)S(1)}, u32[]{:S(2)}, u32[]{:S(2)}) collective-permute-start(bf16[64,3712]{1,0:T(8,128)(2,1)S(1)} %slice.67), channel_id=1, source_target_pairs={{0,72},{4,52},{16,88},{20,4},{32,104},{36,20},{48,120},{52,36},{8,... | collective-permute-start | bytes 1425416 | tf_op jit(solution)/shard_map/ppermute | solution.py:32
  33.0 1.3 fusion.12
  35.8 1.3 fusion.8
  37.2 1.3 fusion.11
  38.5 1.3 fusion.7
  39.9 1.4 %collective-permute-start.22 = (bf16[128,3712]{1,0:T(8,128)(2,1)S(1)}, bf16[128,3712]{1,0:T(8,128)(2,1)S(1)}, u32[]{:S(2)}, u32[]{:S(2)}) collective-permute-start(bf16[128,3712]{1,0:T(8,128)(2,1)S(1)} %constant_dynamic-update-slice_fusion.1), channel_id=1, source_target_pairs={{0,4},{4,0},{16,20},{20,16},{32,36},{36,32},{48,52},{52,48},{8,12}... | collective-permute-start | bytes 2850824 | tf_op jit(solution)/shard_map/ppermute | solution.py:36
  44.3 2.6 %collective-permute-start.8 = (bf16[2,128,2048]{2,1,0:T(8,128)(2,1)S(1)}, bf16[2,128,2048]{2,1,0:T(8,128)(2,1)S(1)}, u32[]{:S(2)}, u32[]{:S(2)}) collective-permute-start(bf16[2,128,2048]{2,1,0:T(8,128)(2,1)S(1)} %pad_maximum_fusion.1), channel_id=1, source_target_pairs={{0,1},{1,0},{2,3},{3,2},{4,7},{5,6},{6,5},{7,4},{8,9},{9,8},{10,11... | collective-permute-start | bytes 3145736 | tf_op jit(solution)/shard_map/ppermute | solution.py:71
  47.4 11.9 %collective-permute-done.8 = bf16[2,128,2048]{2,1,0:T(8,128)(2,1)S(1)} collective-permute-done((bf16[2,128,2048]{2,1,0:T(8,128)(2,1)S(1)}, bf16[2,128,2048]{2,1,0:T(8,128)(2,1)S(1)}, u32[]{:S(2)}, u32[]{:S(2)}) %collective-permute-start.8) | collective-permute-done | bytes 1048608 | tf_op jit(solution)/shard_map/ppermute | solution.py:71
  59.9 7.9 %collective-permute-done.9 = bf16[128,2048]{1,0:T(8,128)(2,1)S(1)} collective-permute-done((bf16[128,2048]{1,0:T(8,128)(2,1)S(1)}, bf16[128,2048]{1,0:T(8,128)(2,1)S(1)}, u32[]{:S(2)}, u32[]{:S(2)}) %collective-permute-start.9) | collective-permute-done | bytes 524320 | tf_op jit(solution)/shard_map/ppermute | solution.py:71
  68.8 2.4 %collective-permute-start.13 = (bf16[128,2048]{1,0:T(8,128)(2,1)S(1)}, bf16[128,2048]{1,0:T(8,128)(2,1)S(1)}, u32[]{:S(2)}, u32[]{:S(2)}) collective-permute-start(bf16[128,2048]{1,0:T(8,128)(2,1)S(1)} %get-tuple-element.35), channel_id=1, source_target_pairs={{0,3},{1,0},{2,1},{3,2},{4,7},{5,4},{6,5},{7,6},{8,11},{9,8},{10,9... | collective-permute-start | bytes 1572872 | tf_op jit(solution)/shard_map/ppermute | solution.py:31
  71.5 2.9 %collective-permute-start.10 = (bf16[2,2,32,1024]{3,2,1,0:T(8,128)(2,1)S(1)}, bf16[2,2,32,1024]{3,2,1,0:T(8,128)(2,1)S(1)}, u32[]{:S(2)}, u32[]{:S(2)}) collective-permute-start(bf16[2,2,32,1024]{3,2,1,0:T(8,128)(2,1)S(1)} %bitcast_select_fusion), channel_id=1, source_target_pairs={{0,4},{4,0},{16,20},{20,16},{32,36},{36,32},{48,52},{52,48},{8,12}... | collective-permute-start | bytes 786440 | tf_op jit(solution)/shard_map/ppermute | solution.py:36
  74.4 6.6 %shard_map.59 = bf16[2048,3712]{1,0:T(8,128)(2,1)S(1)} custom-call(bf16[16,128]{1,0:T(8,128)(2,1)S(1)} %slice.89.after_ref, bf16[3712,1024]{1,0:T(8,128)(2,1)S(1)} %bitcast.147, bf16[3712,1024]{1,0:T(8,128)(2,1)S(1)} %shard_map.58.refs_1_), custom_call_target="tpu_custom_call" | custom-call | bytes 30408704 | tf_op jit(solution)/shard_map/pallas_call | solution.py:95
  81.3 2.3 %collective-permute-start.15 = (bf16[64,2048]{1,0:T(8,128)(2,1)S(1)}, bf16[64,2048]{1,0:T(8,128)(2,1)S(1)}, u32[]{:S(2)}, u32[]{:S(2)}) collective-permute-start(bf16[64,2048]{1,0:T(8,128)(2,1)S(1)} %slice.74), channel_id=1, source_target_pairs={{0,3},{1,0},{2,1},{3,2},{4,7},{5,4},{6,5},{7,6},{8,11},{9,8},{10,9... | collective-permute-start | bytes 786440 | tf_op jit(solution)/shard_map/ppermute | solution.py:31
  83.9 3.1 %collective-permute-done.15 = bf16[64,2048]{1,0:T(8,128)(2,1)S(1)} collective-permute-done((bf16[64,2048]{1,0:T(8,128)(2,1)S(1)}, bf16[64,2048]{1,0:T(8,128)(2,1)S(1)}, u32[]{:S(2)}, u32[]{:S(2)}) %collective-permute-start.15) | collective-permute-done | bytes 262176 | tf_op jit(solution)/shard_map/ppermute | solution.py:31
  86.9 3.2 %collective-permute-done.14 = bf16[64,2048]{1,0:T(8,128)(2,1)S(1)} collective-permute-done((bf16[64,2048]{1,0:T(8,128)(2,1)S(1)}, bf16[64,2048]{1,0:T(8,128)(2,1)S(1)}, u32[]{:S(2)}, u32[]{:S(2)}) %collective-permute-start.14) | collective-permute-done | bytes 262176 | tf_op jit(solution)/shard_map/ppermute | solution.py:31
  90.3 2.2 %convolution_convert_fusion.1 = bf16[128,3712]{1,0:T(8,128)(2,1)S(1)} fusion(bf16[128,2048]{1,0:T(8,128)(2,1)S(1)} %bitcast.172, bf16[2048,3712]{1,0:T(8,128)(2,1)S(1)} %shard_map.59), kind=kOutput, calls=%fused_computation.9 | convolution fusion | flops 1946632192 | bytes 16678912 | tf_op jit(solution)/shard_map/dot_general | solution.py:206
  92.6 1.4 %collective-permute-start.17 = (bf16[64,3712]{1,0:T(8,128)(2,1)S(1)}, bf16[64,3712]{1,0:T(8,128)(2,1)S(1)}, u32[]{:S(2)}, u32[]{:S(2)}) collective-permute-start(bf16[64,3712]{1,0:T(8,128)(2,1)S(1)} %get-tuple-element.53), channel_id=1, source_target_pairs={{0,72},{4,52},{16,88},{20,4},{32,104},{36,20},{48,120},{52,36},{8,... | collective-permute-start | bytes 1425416 | tf_op jit(solution)/shard_map/ppermute | solution.py:32
  94.5 6.0 %collective-permute-start.18 = (bf16[512,1024]{1,0:T(8,128)(2,1)S(1)}, bf16[512,1024]{1,0:T(8,128)(2,1)S(1)}, u32[]{:S(2)}, u32[]{:S(2)}) collective-permute-start(bf16[512,1024]{1,0:T(8,128)(2,1)S(1)} %get-tuple-element.44), channel_id=1, source_target_pairs={{0,4},{4,0},{16,20},{20,16},{32,36},{36,32},{48,52},{52,48},{8,12}... | collective-permute-start | bytes 3145736 | tf_op jit(solution)/shard_map/ppermute | solution.py:36
  100.6 9.5 %fusion.46 = (bf16[384,3712]{1,0:T(8,128)(2,1)S(1)}, f32[384,3712]{1,0:T(8,128)S(1)}) fusion(bf16[2048,3712]{1,0:T(8,128)(2,1)} %copy-done, bf16[128,2048]{1,0:T(8,128)(2,1)S(1)} %bitcast.174, bf16[128,2048]{1,0:T(8,128)(2,1)S(1)} %bitcast.175, bf16[128,2048]{1,0:T(8,128)(2,1)S(1)} %bitcast.173), kind=kOutput, calls=%fused_computation.109 | convolution fusion | flops 5844615168 | bytes 25329664 | tf_op jit(solution)/shard_map/dot_general | solution.py:210
  111.0 2.7 %collective-permute-start.24 = (bf16[128,3712]{1,0:T(8,128)(2,1)S(1)}, bf16[128,3712]{1,0:T(8,128)(2,1)S(1)}, u32[]{:S(2)}, u32[]{:S(2)}) collective-permute-start(bf16[128,3712]{1,0:T(8,128)(2,1)S(1)} %get-tuple-element.30), channel_id=1, source_target_pairs={{0,72},{4,52},{16,88},{20,4},{32,104},{36,20},{48,120},{52,36},{8,... | collective-permute-start | bytes 2850824 | tf_op jit(solution)/shard_map/ppermute | solution.py:32
  113.6 10.5 %convolution_convert_fusion = bf16[3712,1024]{1,0:T(8,128)(2,1)} fusion(bf16[1024,3712]{1,0:T(8,128)(2,1)S(1)} %bitcast.167, bf16[1024,1024]{1,0:T(8,128)(2,1)S(1)} %pad_maximum_fusion), kind=kOutput, calls=%fused_computation | convolution fusion | flops 7788429312 | bytes 17301504 | tf_op jit(solution)/shard_map/dot_general | solution.py:220
  125.5 1.8 %collective-permute-start.27 = (bf16[32,3712]{1,0:T(8,128)(2,1)S(1)}, bf16[32,3712]{1,0:T(8,128)(2,1)S(1)}, u32[]{:S(2)}, u32[]{:S(2)}) collective-permute-start(bf16[32,3712]{1,0:T(8,128)(2,1)S(1)} %get-tuple-element.49), channel_id=1, source_target_pairs={{0,32},{4,68},{16,48},{20,84},{32,0},{36,100},{48,16},{52,116},{8,... | collective-permute-start | bytes 712712 | tf_op jit(solution)/shard_map/ppermute | solution.py:32
  127.3 1.3 collective-permute-start.26
  130.1 2.3 %collective-permute-done.27 = bf16[32,3712]{1,0:T(8,128)(2,1)S(1)} collective-permute-done((bf16[32,3712]{1,0:T(8,128)(2,1)S(1)}, bf16[32,3712]{1,0:T(8,128)(2,1)S(1)}, u32[]{:S(2)}, u32[]{:S(2)}) %collective-permute-start.27) | collective-permute-done | bytes 237600 | tf_op jit(solution)/shard_map/ppermute | solution.py:32
  132.3 3.2 %collective-permute-done.26 = bf16[32,3712]{1,0:T(8,128)(2,1)S(1)} collective-permute-done((bf16[32,3712]{1,0:T(8,128)(2,1)S(1)}, bf16[32,3712]{1,0:T(8,128)(2,1)S(1)}, u32[]{:S(2)}, u32[]{:S(2)}) %collective-permute-start.26) | collective-permute-done | bytes 237600 | tf_op jit(solution)/shard_map/ppermute | solution.py:32
  (100 shorter events, 19.6 us)
Async XLA Ops:
  0.6 23.2 %collective-permute-start.3 = (bf16[3712,1024]{1,0:T(8,128)(2,1)}, bf16[3712,1024]{1,0:T(8,128)(2,1)}, u32[]{:S(2)}, u32[]{:S(2)}) collective-permute-start(bf16[3712,1024]{1,0:T(8,128)(2,1)} %refs_0_.1), channel_id=1, source_target_pairs={{0,4},{4,0},{16,20},{20,16},{32,36},{36,32},{48,52},{52,48},{8,12}... | collective-permute-start | bytes 22806536 | tf_op jit(solution)/shard_map/ppermute | solution.py:36
  2.1 8.4 %collective-permute-start = (bf16[32,3712]{1,0:T(8,128)(2,1)}, bf16[32,3712]{1,0:T(8,128)(2,1)S(1)}, u32[]{:S(2)}, u32[]{:S(2)}) collective-permute-start(bf16[32,3712]{1,0:T(8,128)(2,1)} %param.3), channel_id=1, source_target_pairs={{0,32},{4,68},{16,48},{20,84},{32,0},{36,100},{48,16},{52,116},{8,... | collective-permute-start | bytes 712712 | tf_op jit(solution)/shard_map/ppermute | solution.py:32
  5.8 7.3 %collective-permute-start.1 = (bf16[32,3712]{1,0:T(8,128)(2,1)}, bf16[32,3712]{1,0:T(8,128)(2,1)S(1)}, u32[]{:S(2)}, u32[]{:S(2)}) collective-permute-start(bf16[32,3712]{1,0:T(8,128)(2,1)} %param.3), channel_id=1, source_target_pairs={{0,48},{4,76},{16,0},{20,92},{32,16},{36,108},{48,32},{52,124},{8,... | collective-permute-start | bytes 712712 | tf_op jit(solution)/shard_map/ppermute | solution.py:32
  6.2 6.9 %collective-permute-start.2 = (bf16[32,3712]{1,0:T(8,128)(2,1)}, bf16[32,3712]{1,0:T(8,128)(2,1)S(1)}, u32[]{:S(2)}, u32[]{:S(2)}) collective-permute-start(bf16[32,3712]{1,0:T(8,128)(2,1)} %param.3), channel_id=1, source_target_pairs={{0,16},{4,12},{16,32},{20,28},{32,48},{36,44},{48,0},{52,60},{8,24... | collective-permute-start | bytes 712712 | tf_op jit(solution)/shard_map/ppermute | solution.py:32
  8.4 15.2 %collective-permute-start.11 = (bf16[2,2,32,1024]{3,2,1,0:T(8,128)(2,1)S(1)}, bf16[2,2,32,1024]{3,2,1,0:T(8,128)(2,1)S(1)}, u32[]{:S(2)}, u32[]{:S(2)}) collective-permute-start(bf16[2,2,32,1024]{3,2,1,0:T(8,128)(2,1)S(1)} %get-tuple-element.58), channel_id=1, source_target_pairs={{0,4},{4,0},{16,20},{20,16},{32,36},{36,32},{48,52},{52,48},{8,12}... | collective-permute-start | bytes 786440 | tf_op jit(solution)/shard_map/ppermute | solution.py:36
  13.2 16.4 %collective-permute-start.4 = (bf16[128,3712]{1,0:T(8,128)(2,1)S(1)}, bf16[128,3712]{1,0:T(8,128)(2,1)S(1)}, u32[]{:S(2)}, u32[]{:S(2)}) collective-permute-start(bf16[128,3712]{1,0:T(8,128)(2,1)S(1)} %bitcast.154), channel_id=1, source_target_pairs={{0,8},{4,20},{16,24},{20,36},{32,40},{36,52},{48,56},{52,4},{8,64}... | collective-permute-start | bytes 2850824 | tf_op jit(solution)/shard_map/ppermute | solution.py:32
  14.3 15.3 %collective-permute-start.5 = (bf16[128,3712]{1,0:T(8,128)(2,1)S(1)}, bf16[128,3712]{1,0:T(8,128)(2,1)S(1)}, u32[]{:S(2)}, u32[]{:S(2)}) collective-permute-start(bf16[128,3712]{1,0:T(8,128)(2,1)S(1)} %bitcast.155), channel_id=1, source_target_pairs={{0,72},{4,52},{16,88},{20,4},{32,104},{36,20},{48,120},{52,36},{8,... | collective-permute-start | bytes 2850824 | tf_op jit(solution)/shard_map/ppermute | solution.py:32
  16.0 7.7 %collective-permute-start.19 = (bf16[128,3712]{1,0:T(8,128)(2,1)S(1)}, bf16[128,3712]{1,0:T(8,128)(2,1)S(1)}, u32[]{:S(2)}, u32[]{:S(2)}) collective-permute-start(bf16[128,3712]{1,0:T(8,128)(2,1)S(1)} %bitcast.156), channel_id=1, source_target_pairs={{0,4},{4,0},{16,20},{20,16},{32,36},{36,32},{48,52},{52,48},{8,12}... | collective-permute-start | bytes 2850824 | tf_op jit(solution)/shard_map/ppermute | solution.py:36
  23.7 9.4 %slice-start = ((s8[7602176]{0:T(1024)(128)(4,1)}), s8[4194304]{0:T(1024)(128)(4,1)S(1)}, s32[]{:S(2)}) async-start(s8[7602176]{0:T(1024)(128)(4,1)} %bitcast.146), calls=%async_computation | async-start | bytes 8388608
  23.8 9.2 %slice-start.1 = ((s8[7602176]{0:T(1024)(128)(4,1)}), s8[3407872]{0:T(1024)(128)(4,1)S(1)}, s32[]{:S(2)}) async-start(s8[7602176]{0:T(1024)(128)(4,1)} %bitcast.146), calls=%async_computation.1 | async-start | bytes 6815744
  29.7 17.2 %collective-permute-start.20 = (bf16[128,3712]{1,0:T(8,128)(2,1)S(1)}, bf16[128,3712]{1,0:T(8,128)(2,1)S(1)}, u32[]{:S(2)}, u32[]{:S(2)}) collective-permute-start(bf16[128,3712]{1,0:T(8,128)(2,1)S(1)} %collective-permute-done.4), channel_id=1, source_target_pairs={{0,4},{4,0},{16,20},{20,16},{32,36},{36,32},{48,52},{52,48},{8,12}... | collective-permute-start | bytes 2850824 | tf_op jit(solution)/shard_map/ppermute | solution.py:36
  30.1 17.0 %collective-permute-start.21 = (bf16[128,3712]{1,0:T(8,128)(2,1)S(1)}, bf16[128,3712]{1,0:T(8,128)(2,1)S(1)}, u32[]{:S(2)}, u32[]{:S(2)}) collective-permute-start(bf16[128,3712]{1,0:T(8,128)(2,1)S(1)} %collective-permute-done.5), channel_id=1, source_target_pairs={{0,4},{4,0},{16,20},{20,16},{32,36},{36,32},{48,52},{52,48},{8,12}... | collective-permute-start | bytes 2850824 | tf_op jit(solution)/shard_map/ppermute | solution.py:36
  30.4 9.4 %collective-permute-start.6 = (bf16[64,3712]{1,0:T(8,128)(2,1)S(1)}, bf16[64,3712]{1,0:T(8,128)(2,1)S(1)}, u32[]{:S(2)}, u32[]{:S(2)}) collective-permute-start(bf16[64,3712]{1,0:T(8,128)(2,1)S(1)} %slice.66), channel_id=1, source_target_pairs={{0,8},{4,20},{16,24},{20,36},{32,40},{36,52},{48,56},{52,4},{8,64}... | collective-permute-start | bytes 1425416 | tf_op jit(solution)/shard_map/ppermute | solution.py:32
  30.4 9.5 %collective-permute-start.7 = (bf16[64,3712]{1,0:T(8,128)(2,1)S(1)}, bf16[64,3712]{1,0:T(8,128)(2,1)S(1)}, u32[]{:S(2)}, u32[]{:S(2)}) collective-permute-start(bf16[64,3712]{1,0:T(8,128)(2,1)S(1)} %slice.67), channel_id=1, source_target_pairs={{0,72},{4,52},{16,88},{20,4},{32,104},{36,20},{48,120},{52,36},{8,... | collective-permute-start | bytes 1425416 | tf_op jit(solution)/shard_map/ppermute | solution.py:32
  39.9 19.9 %collective-permute-start.22 = (bf16[128,3712]{1,0:T(8,128)(2,1)S(1)}, bf16[128,3712]{1,0:T(8,128)(2,1)S(1)}, u32[]{:S(2)}, u32[]{:S(2)}) collective-permute-start(bf16[128,3712]{1,0:T(8,128)(2,1)S(1)} %constant_dynamic-update-slice_fusion.1), channel_id=1, source_target_pairs={{0,4},{4,0},{16,20},{20,16},{32,36},{36,32},{48,52},{52,48},{8,12}... | collective-permute-start | bytes 2850824 | tf_op jit(solution)/shard_map/ppermute | solution.py:36
  44.3 14.9 %collective-permute-start.8 = (bf16[2,128,2048]{2,1,0:T(8,128)(2,1)S(1)}, bf16[2,128,2048]{2,1,0:T(8,128)(2,1)S(1)}, u32[]{:S(2)}, u32[]{:S(2)}) collective-permute-start(bf16[2,128,2048]{2,1,0:T(8,128)(2,1)S(1)} %pad_maximum_fusion.1), channel_id=1, source_target_pairs={{0,1},{1,0},{2,3},{3,2},{4,7},{5,6},{6,5},{7,4},{8,9},{9,8},{10,11... | collective-permute-start | bytes 3145736 | tf_op jit(solution)/shard_map/ppermute | solution.py:71
  59.4 8.4 %collective-permute-start.9 = (bf16[128,2048]{1,0:T(8,128)(2,1)S(1)}, bf16[128,2048]{1,0:T(8,128)(2,1)S(1)}, u32[]{:S(2)}, u32[]{:S(2)}) collective-permute-start(bf16[128,2048]{1,0:T(8,128)(2,1)S(1)} %fusion.33), channel_id=1, source_target_pairs={{0,3},{1,2},{2,1},{3,0},{4,5},{5,4},{6,7},{7,6},{8,11},{9,10},{10,... | collective-permute-start | bytes 1572872 | tf_op jit(solution)/shard_map/ppermute | solution.py:71
  68.5 12.8 %collective-permute-start.12 = (bf16[128,2048]{1,0:T(8,128)(2,1)S(1)}, bf16[128,2048]{1,0:T(8,128)(2,1)S(1)}, u32[]{:S(2)}, u32[]{:S(2)}) collective-permute-start(bf16[128,2048]{1,0:T(8,128)(2,1)S(1)} %get-tuple-element.35), channel_id=1, source_target_pairs={{0,1},{1,2},{2,3},{3,0},{4,5},{5,6},{6,7},{7,4},{8,9},{9,10},{10,1... | collective-permute-start | bytes 1572872 | tf_op jit(solution)/shard_map/ppermute | solution.py:31
  68.8 12.5 %collective-permute-start.13 = (bf16[128,2048]{1,0:T(8,128)(2,1)S(1)}, bf16[128,2048]{1,0:T(8,128)(2,1)S(1)}, u32[]{:S(2)}, u32[]{:S(2)}) collective-permute-start(bf16[128,2048]{1,0:T(8,128)(2,1)S(1)} %get-tuple-element.35), channel_id=1, source_target_pairs={{0,3},{1,0},{2,1},{3,2},{4,7},{5,4},{6,5},{7,6},{8,11},{9,8},{10,9... | collective-permute-start | bytes 1572872 | tf_op jit(solution)/shard_map/ppermute | solution.py:31
  71.5 57.6 %collective-permute-start.10 = (bf16[2,2,32,1024]{3,2,1,0:T(8,128)(2,1)S(1)}, bf16[2,2,32,1024]{3,2,1,0:T(8,128)(2,1)S(1)}, u32[]{:S(2)}, u32[]{:S(2)}) collective-permute-start(bf16[2,2,32,1024]{3,2,1,0:T(8,128)(2,1)S(1)} %bitcast_select_fusion), channel_id=1, source_target_pairs={{0,4},{4,0},{16,20},{20,16},{32,36},{36,32},{48,52},{52,48},{8,12}... | collective-permute-start | bytes 786440 | tf_op jit(solution)/shard_map/ppermute | solution.py:36
  80.9 11.6 %copy-start = (bf16[2048,3712]{1,0:T(8,128)(2,1)}, bf16[2048,3712]{1,0:T(8,128)(2,1)S(1)}, u32[]{:S(2)}) copy-start(bf16[2048,3712]{1,0:T(8,128)(2,1)S(1)} %shard_map.59) | copy-start | bytes 45613060
  81.3 5.6 %collective-permute-start.15 = (bf16[64,2048]{1,0:T(8,128)(2,1)S(1)}, bf16[64,2048]{1,0:T(8,128)(2,1)S(1)}, u32[]{:S(2)}, u32[]{:S(2)}) collective-permute-start(bf16[64,2048]{1,0:T(8,128)(2,1)S(1)} %slice.74), channel_id=1, source_target_pairs={{0,3},{1,0},{2,1},{3,2},{4,7},{5,4},{6,5},{7,6},{8,11},{9,8},{10,9... | collective-permute-start | bytes 786440 | tf_op jit(solution)/shard_map/ppermute | solution.py:31
  83.6 6.5 %collective-permute-start.14 = (bf16[64,2048]{1,0:T(8,128)(2,1)S(1)}, bf16[64,2048]{1,0:T(8,128)(2,1)S(1)}, u32[]{:S(2)}, u32[]{:S(2)}) collective-permute-start(bf16[64,2048]{1,0:T(8,128)(2,1)S(1)} %slice.73), channel_id=1, source_target_pairs={{0,1},{1,2},{2,3},{3,0},{4,5},{5,6},{6,7},{7,4},{8,9},{9,10},{10,1... | collective-permute-start | bytes 786440 | tf_op jit(solution)/shard_map/ppermute | solution.py:31
  92.6 17.8 %collective-permute-start.17 = (bf16[64,3712]{1,0:T(8,128)(2,1)S(1)}, bf16[64,3712]{1,0:T(8,128)(2,1)S(1)}, u32[]{:S(2)}, u32[]{:S(2)}) collective-permute-start(bf16[64,3712]{1,0:T(8,128)(2,1)S(1)} %get-tuple-element.53), channel_id=1, source_target_pairs={{0,72},{4,52},{16,88},{20,4},{32,104},{36,20},{48,120},{52,36},{8,... | collective-permute-start | bytes 1425416 | tf_op jit(solution)/shard_map/ppermute | solution.py:32
  94.0 16.4 %collective-permute-start.16 = (bf16[64,3712]{1,0:T(8,128)(2,1)S(1)}, bf16[64,3712]{1,0:T(8,128)(2,1)S(1)}, u32[]{:S(2)}, u32[]{:S(2)}) collective-permute-start(bf16[64,3712]{1,0:T(8,128)(2,1)S(1)} %get-tuple-element.54), channel_id=1, source_target_pairs={{0,8},{4,20},{16,24},{20,36},{32,40},{36,52},{48,56},{52,4},{8,64}... | collective-permute-start | bytes 1425416 | tf_op jit(solution)/shard_map/ppermute | solution.py:32
  94.5 16.2 %collective-permute-start.18 = (bf16[512,1024]{1,0:T(8,128)(2,1)S(1)}, bf16[512,1024]{1,0:T(8,128)(2,1)S(1)}, u32[]{:S(2)}, u32[]{:S(2)}) collective-permute-start(bf16[512,1024]{1,0:T(8,128)(2,1)S(1)} %get-tuple-element.44), channel_id=1, source_target_pairs={{0,4},{4,0},{16,20},{20,16},{32,36},{36,32},{48,52},{52,48},{8,12}... | collective-permute-start | bytes 3145736 | tf_op jit(solution)/shard_map/ppermute | solution.py:36
  110.9 14.2 %collective-permute-start.23 = (bf16[128,3712]{1,0:T(8,128)(2,1)S(1)}, bf16[128,3712]{1,0:T(8,128)(2,1)S(1)}, u32[]{:S(2)}, u32[]{:S(2)}) collective-permute-start(bf16[128,3712]{1,0:T(8,128)(2,1)S(1)} %get-tuple-element.29), channel_id=1, source_target_pairs={{0,8},{4,20},{16,24},{20,36},{32,40},{36,52},{48,56},{52,4},{8,64}... | collective-permute-start | bytes 2850824 | tf_op jit(solution)/shard_map/ppermute | solution.py:32
  111.0 14.1 %collective-permute-start.24 = (bf16[128,3712]{1,0:T(8,128)(2,1)S(1)}, bf16[128,3712]{1,0:T(8,128)(2,1)S(1)}, u32[]{:S(2)}, u32[]{:S(2)}) collective-permute-start(bf16[128,3712]{1,0:T(8,128)(2,1)S(1)} %get-tuple-element.30), channel_id=1, source_target_pairs={{0,72},{4,52},{16,88},{20,4},{32,104},{36,20},{48,120},{52,36},{8,... | collective-permute-start | bytes 2850824 | tf_op jit(solution)/shard_map/ppermute | solution.py:32
  125.5 6.8 %collective-permute-start.27 = (bf16[32,3712]{1,0:T(8,128)(2,1)S(1)}, bf16[32,3712]{1,0:T(8,128)(2,1)S(1)}, u32[]{:S(2)}, u32[]{:S(2)}) collective-permute-start(bf16[32,3712]{1,0:T(8,128)(2,1)S(1)} %get-tuple-element.49), channel_id=1, source_target_pairs={{0,32},{4,68},{16,48},{20,84},{32,0},{36,100},{48,16},{52,116},{8,... | collective-permute-start | bytes 712712 | tf_op jit(solution)/shard_map/ppermute | solution.py:32
  127.3 8.2 %collective-permute-start.26 = (bf16[32,3712]{1,0:T(8,128)(2,1)S(1)}, bf16[32,3712]{1,0:T(8,128)(2,1)S(1)}, u32[]{:S(2)}, u32[]{:S(2)}) collective-permute-start(bf16[32,3712]{1,0:T(8,128)(2,1)S(1)} %get-tuple-element.50), channel_id=1, source_target_pairs={{0,48},{4,76},{16,0},{20,92},{32,16},{36,108},{48,32},{52,124},{8,... | collective-permute-start | bytes 712712 | tf_op jit(solution)/shard_map/ppermute | solution.py:32
  128.6 6.9 %collective-permute-start.25 = (bf16[32,3712]{1,0:T(8,128)(2,1)S(1)}, bf16[32,3712]{1,0:T(8,128)(2,1)S(1)}, u32[]{:S(2)}, u32[]{:S(2)}) collective-permute-start(bf16[32,3712]{1,0:T(8,128)(2,1)S(1)} %get-tuple-element.48), channel_id=1, source_target_pairs={{0,16},{4,12},{16,32},{20,28},{32,48},{36,44},{48,0},{52,60},{8,24... | collective-permute-start | bytes 712712 | tf_op jit(solution)/shard_map/ppermute | solution.py:32
